TPU v7x, 32 devices: a whole 2x2x4 slice. The times are simulated.
32 devices in a mesh: space: 4 (over z), mode: 8 (over y, x, core).
Axes of the slice: x: 2, y: 2, z: 4, core: 2. Of those that a mesh axis runs over, the one named last changes fastest.
Arguments:
- sqrt_factors: bfloat16 [512, 3, 192, 512], P('mode', None, 'space'), may hold values from -10 to 10
- model_error: bfloat16 [256, 3, 192, 512], P(None, None, ('space', 'mode')), may hold values from -6 to 6
- water_depth: float32 [192, 512], P('space'), may hold values from 0.5 to 2
- sea_mask: int32 [192, 512], P('space'), may hold values 0 or 1
- givens_transform: bfloat16 [768, 512], replicated, may hold values from -0.2 to 1.2
Outputs:
- reduced_modes: bfloat16 [512, 3, 192, 512], P('mode', None, 'space')
- gram_matrix: float32 [768, 768], P(('space', 'mode'))
- inflation: float32 [], replicated
All inputs are finite; a program needn't handle non-finite values. No bound on the sum of `sea_mask` on one device may be relied on, other than what follows from the above.
Results may differ from a plain program's by a relative error of at most 0.0049.
Values may be sent and summed in bfloat16 or wider, within the bound.
No kernel may reach another device: no remote copies, remote signals or barrier semaphores. Data moves between devices by JAX's collectives and lax.ppermute only.
A program may use at most 128 MiB of HBM per device.

v0:
```python
import functools

import jax
import jax.numpy as jnp
import numpy as np
from jax import lax
from jax.experimental import pallas as pl
from jax.experimental.pallas import tpu as pltpu
from jax.sharding import PartitionSpec as P

flux_coef = 0.2
slope_coef = 0.2
turn_coef = 0.1
keep_coef = 0.95

GROUP = 16
HALO = 4
LANES = 128
VMEM_BYTES = 48 * 1024 * 1024


def column_diff(tiles):
    lane = lax.broadcasted_iota(jnp.int32, tiles[0].shape, 1)
    from_left = [pltpu.roll(tile, 1, 1) for tile in tiles]
    from_right = [pltpu.roll(tile, LANES - 1, 1) for tile in tiles]
    zero = jnp.zeros_like(tiles[0])
    out = []
    for t in range(len(tiles)):
        left = from_left[t - 1] if t > 0 else zero
        right = from_right[t + 1] if t + 1 < len(tiles) else zero
        previous = jnp.where(lane == 0, left, from_left[t])
        following = jnp.where(lane == LANES - 1, right, from_right[t])
        out.append(following - previous)
    return out


def swap_matrix(inner, outer):
    place = np.arange(inner * outer).reshape(outer, inner).T.reshape(-1)
    matrix = np.zeros((inner * outer, inner * outer), np.float32)
    matrix[np.arange(inner * outer), place] = 1.0
    return jnp.asarray(matrix, jnp.bfloat16)


def in_hbm(shape, dtype):
    return pltpu.HBM(shape, dtype)


def cut_edges_kernel(fixed, *refs):
    first_ref, last_ref = refs[:2]
    out_first, out_last = refs[-2:]
    group, fields = first_ref.shape[:2]
    for ref, out, low in ((first_ref, out_first, 0), (last_ref, out_last, GROUP - HALO)):
        for m in range(group):
            for field in range(fields):
                edge = ref[m, field].astype(jnp.float32)[low:low + HALO]
                out[m * fields + field] = edge.astype(jnp.bfloat16)
    if fixed:
        depth_ref, mask_ref = refs[2:4]
        for out, low in ((out_first, 0), (out_last, depth_ref.shape[0] - HALO)):
            rest = depth_ref[low:low + HALO]
            for piece in range(3):
                part = rest.astype(jnp.bfloat16)
                out[group * fields + piece] = part
                rest = rest - part.astype(jnp.float32)
            out[group * fields + 3] = mask_ref[low:low + HALO].astype(jnp.float32).astype(jnp.bfloat16)


def cut_edges(first, groups, factors, fixed):
    _, fields, rows, width = factors.shape
    size = GROUP * groups if fixed else GROUP
    steps = 1 if fixed else groups
    count = size * steps * fields + (4 if fixed else 0)
    block = size * fields + (4 if fixed else 0)
    place = jax.ShapeDtypeStruct if fixed else in_hbm
    out = place((count, HALO, width), jnp.bfloat16)
    return pl.pallas_call(
        functools.partial(cut_edges_kernel, bool(fixed)),
        grid=(steps,),
        out_shape=(out, out),
        in_specs=[
            pl.BlockSpec((size, fields, GROUP, width), lambda i: (first // (size // GROUP) + i, 0, 0, 0)),
            pl.BlockSpec((size, fields, GROUP, width),
                         lambda i: (first // (size // GROUP) + i, 0, rows // GROUP - 1, 0)),
        ] + [pl.BlockSpec(value.shape, lambda i: (0, 0)) for value in fixed],
        out_specs=[pl.BlockSpec((block, HALO, width), lambda i: (i, 0, 0))] * 2,
        compiler_params=pltpu.CompilerParams(vmem_limit_bytes=VMEM_BYTES),
        cost_estimate=pl.CostEstimate(
            flops=0, bytes_accessed=5 * count * HALO * width * 2, transcendentals=0
        ),
        name="cut_edges",
    )(factors, factors, *fixed)


def block_of(count):
    return max(size for size in range(1, 55) if count % size == 0)


def forecast_kernel(x_ref, low_ref, high_ref, low_static, high_static, depth_ref, mask_ref,
                    swap_ref, swap_ends_ref, *refs):
    out_ref, cells, ends, depth, wet, surf1, east1, north1, surf2 = refs[-9:]
    _, fields, rows, width = x_ref.shape
    tiles = width // LANES
    spots = [slice(t * LANES, (t + 1) * LANES) for t in range(tiles)]

    ends[:, :HALO] = low_ref[...].astype(jnp.float32)
    ends[:, HALO:] = high_ref[...].astype(jnp.float32)
    for field in range(fields):
        for top in range(0, rows, GROUP):
            block = x_ref[:, field, top:top + GROUP, :].reshape(GROUP * GROUP, width)
            block = jnp.dot(swap_ref[...], block, preferred_element_type=jnp.float32)
            block = block * slope_coef if field == 0 else block
            cells[field, HALO + top:HALO + top + GROUP] = block.reshape(GROUP, GROUP, width)
        block = jnp.concatenate([ends[m * fields + field] for m in range(GROUP)], axis=0)
        block = jnp.dot(
            swap_ends_ref[...], block.astype(jnp.bfloat16), preferred_element_type=jnp.float32
        ).reshape(2 * HALO, GROUP, width)
        block = block * slope_coef if field == 0 else block
        cells[field, :HALO] = block[:HALO]
        cells[field, HALO + rows:] = block[HALO:]

    def place_static(place, depth_row, wet_row):
        depth[place] = jnp.broadcast_to(flux_coef * slope_coef * depth_row, (8, width))
        wet[place] = jnp.broadcast_to(wet_row, (8, width))

    for static, first in ((low_static, 0), (high_static, HALO + rows)):
        value = static[...].astype(jnp.float32)
        level = value[0] + value[1] + value[2]
        for j in range(HALO):
            place_static(first + j, level[j:j + 1], value[3, j:j + 1])
    for top in range(0, rows, 8):
        level = depth_ref[top:top + 8]
        sea = mask_ref[top:top + 8].astype(jnp.float32)
        for j in range(8):
            place_static(HALO + top + j, level[j:j + 1], sea[j:j + 1])

    def get(ref, i):
        return [ref[i, :, spot] for spot in spots]

    def get_field(field, i):
        return [cells[field, i + HALO, :, spot] for spot in spots]

    def get_static(ref, i):
        parts = [ref[i + HALO, :, spot] for spot in spots]
        return [jnp.concatenate([part] * (GROUP // 8), axis=0) for part in parts]

    def put(ref, i, values):
        for spot, value in zip(spots, values):
            ref[i, :, spot] = value

    def times(one, other):
        return [a * b for a, b in zip(one, other)]

    def over_rows(first, last, body):
        size = block_of(last - first)

        def block(k, carry):
            body(first + k * size, size)
            return carry

        lax.fori_loop(0, (last - first) // size, block, 0)

    def surfaces(i, size, surface_at, east_at, north_at, put_at):
        flux = {j: times(get_static(depth, i + j), north_at(i + j)) for j in (-1, 0)}
        for j in range(size):
            flux[j + 1] = times(get_static(depth, i + j + 1), north_at(i + j + 1))
            sides = column_diff(times(get_static(depth, i + j), east_at(i + j)))
            sea, surface = get_static(wet, i + j), surface_at(i + j)
            put_at(i + j, [
                sea[t] * (surface[t] - (sides[t] + (flux[j + 1][t] - flux[j - 1][t])))
                for t in range(tiles)
            ])

    def flows(i, size, surface_at, east_at, north_at, put_at):
        surface = {j: surface_at(i + j) for j in (-1, 0)}
        for j in range(size):
            surface[j + 1] = surface_at(i + j + 1)
            sides = column_diff(surface[j])
            sea, east, north = get_static(wet, i + j), east_at(i + j), north_at(i + j)
            put_at(i + j, surface[j], [
                sea[t] * (keep_coef * east[t] + turn_coef * north[t] - sides[t])
                for t in range(tiles)
            ], [
                sea[t] * (keep_coef * north[t] - turn_coef * east[t]
                          - (surface[j + 1][t] - surface[j - 1][t]))
                for t in range(tiles)
            ])

    def first_surface(i, size):
        surfaces(
            i, size, lambda r: get_field(0, r), lambda r: get_field(1, r),
            lambda r: get_field(2, r), lambda r, value: put(surf1, r + 3, value),
        )

    def first_flow(i, size):
        def put_flow(r, surface, east, north):
            put(east1, r + 2, east)
            put(north1, r + 2, north)

        flows(
            i, size, lambda r: get(surf1, r + 3), lambda r: get_field(1, r),
            lambda r: get_field(2, r), put_flow,
        )

    def second_surface(i, size):
        surfaces(
            i, size, lambda r: get(surf1, r + 3), lambda r: get(east1, r + 2),
            lambda r: get(north1, r + 2), lambda r, value: put(surf2, r + 1, value),
        )

    def second_flow(i, size):
        def put_out(r, surface, east, north):
            surface = [value * (1.0 / slope_coef) for value in surface]
            for field, values in enumerate((surface, east, north)):
                for spot, value in zip(spots, values):
                    out_ref[r, field, :, spot] = value.astype(jnp.bfloat16)

        flows(
            i, size, lambda r: get(surf2, r + 1), lambda r: get(east1, r + 2),
            lambda r: get(north1, r + 2), put_out,
        )

    over_rows(-3, rows + 3, first_surface)
    over_rows(-2, rows + 2, first_flow)
    over_rows(-1, rows + 1, second_surface)
    over_rows(0, rows, second_flow)


def forecast_groups(first, count, skip, place, whole_count, previous, factors, low, high,
                    static_low, static_high, depth, mask):
    modes, fields, rows, width = factors.shape
    padded = rows + 2 * HALO
    edge = GROUP * fields
    last = static_low.shape[0] // 4 - 1
    swap, swap_ends = swap_matrix(GROUP, GROUP), swap_matrix(2 * HALO, GROUP)

    def rows_of(count):
        return pltpu.VMEM((count, GROUP, width), jnp.float32)

    def whole(value):
        return pl.BlockSpec(value.shape, lambda i: (0,) * value.ndim)

    return pl.pallas_call(
        forecast_kernel,
        grid=(count,),
        out_shape=in_hbm((rows, fields, whole_count * GROUP, width), jnp.bfloat16),
        in_specs=[
            pl.BlockSpec((GROUP, fields, rows, width), lambda i: (first + i, 0, 0, 0)),
            pl.BlockSpec((edge, HALO, width), lambda i: (skip + i, 0, 0)),
            pl.BlockSpec((edge, HALO, width), lambda i: (skip + i, 0, 0)),
            pl.BlockSpec((4, HALO, width), lambda i: (last, 0, 0)),
            pl.BlockSpec((4, HALO, width), lambda i: (last, 0, 0)),
            whole(depth),
            whole(mask),
            whole(swap),
            whole(swap_ends),
        ] + [pl.BlockSpec(memory_space=pltpu.HBM) for _ in previous],
        out_specs=pl.BlockSpec((rows, fields, GROUP, width), lambda i: (0, 0, place + i, 0)),
        input_output_aliases={9: 0} if previous else {},
        scratch_shapes=[
            pltpu.VMEM((fields, padded, GROUP, width), jnp.float32),
            pltpu.VMEM((edge, 2 * HALO, width), jnp.float32),
            pltpu.VMEM((padded, 8, width), jnp.float32),
            pltpu.VMEM((padded, 8, width), jnp.float32),
            rows_of(rows + 6),
            rows_of(rows + 4),
            rows_of(rows + 4),
            rows_of(rows + 2),
        ],
        compiler_params=pltpu.CompilerParams(vmem_limit_bytes=VMEM_BYTES),
        cost_estimate=pl.CostEstimate(
            flops=60 * count * GROUP * rows * width,
            bytes_accessed=2 * 2 * count * GROUP * fields * rows * width,
            transcendentals=0,
        ),
        name="forecast",
    )(factors, low, high, static_low, static_high, depth, mask, swap, swap_ends, *previous)


def all_columns(chunk_refs, fault_ref, j):
    own = [ref[:, j, 0] for ref in chunk_refs]
    joined = jnp.concatenate(own, axis=1)
    return joined.reshape(-1, joined.shape[-1]), fault_ref[0, j]


def rotate_kernel(count, *refs):
    chunk_refs = refs[:count]
    fault_ref, turn_ref, out_ref = refs[count:]
    parts, _, size, modes, width = out_ref.shape
    for j in range(size):
        columns = jnp.concatenate(all_columns(chunk_refs, fault_ref, j), axis=0)
        value = jnp.dot(turn_ref[...], columns, preferred_element_type=jnp.float32)
        out_ref[:, 0, j] = value.astype(jnp.bfloat16).reshape(parts, modes, width)


def by_part(chunks, parts):
    return [c.reshape((parts, c.shape[0] // parts) + c.shape[1:]) for c in chunks]


def rotate_fields(first, fields, chunks, fault, turn, parts):
    width = chunks[0].shape[-1]
    each = chunks[0].shape[0] // parts
    kept = turn.shape[0]
    noise = fault.shape[2]
    modes = kept // parts
    size = 3 if each % 3 == 0 else 1
    views = by_part(chunks, parts)
    return pl.pallas_call(
        functools.partial(rotate_kernel, len(views)),
        grid=(fields, each // size),
        out_shape=in_hbm((parts, fields, each, modes, width), jnp.bfloat16),
        in_specs=[
            pl.BlockSpec((parts, size, 1, v.shape[3], width), lambda f, j: (0, j, first + f, 0, 0))
            for v in views
        ] + [
            pl.BlockSpec((1, size, noise, width), lambda f, j: (first + f, j, 0, 0)),
            pl.BlockSpec(turn.shape, lambda f, j: (0, 0)),
        ],
        out_specs=pl.BlockSpec((parts, 1, size, modes, width), lambda f, j: (0, f, j, 0, 0)),
        compiler_params=pltpu.CompilerParams(vmem_limit_bytes=VMEM_BYTES),
        cost_estimate=pl.CostEstimate(
            flops=2 * fields * each * width * kept * turn.shape[1],
            bytes_accessed=2 * fields * each * width * (kept + turn.shape[1]),
            transcendentals=0,
        ),
        name="rotate",
    )(*views, fault, turn)


def gram_kernel(count, each, devices, *refs):
    chunk_refs = refs[:count]
    fault_ref, turn_ref, half_ref, keep_ref, send_ref, gram_ref = refs[count:]
    pairs = [all_columns(chunk_refs, fault_ref, j) for j in range(each)]
    columns = jnp.concatenate(
        [jnp.concatenate([prior, fault], axis=0) for prior, fault in pairs], axis=1
    )
    value = lax.dot_general(
        columns, columns, (((1,), (1,)), ((), ())), preferred_element_type=jnp.float32
    )
    step = pl.program_id(0)

    @pl.when(step == 0)
    def _():
        gram_ref[...] = value

    @pl.when(step > 0)
    def _():
        gram_ref[...] += value

    @pl.when(step == pl.num_programs(0) - 1)
    def _():
        gram = gram_ref[...]
        size = gram.shape[0]
        row = lax.broadcasted_iota(jnp.int32, gram.shape, 0)
        column = lax.broadcasted_iota(jnp.int32, gram.shape, 1)
        full = jnp.sum(jnp.where(row == column, gram, 0.0))
        turn = turn_ref[...]
        turned = 0.0
        for _ in range(3):
            piece = gram.astype(jnp.bfloat16)
            turned = turned + jnp.dot(turn, piece, preferred_element_type=jnp.float32)
            gram = gram - piece.astype(jnp.float32)
        kept = jnp.sum(turned * turn.astype(jnp.float32))
        own = size // devices
        slot = keep_ref.shape[0] // (devices // 2)
        lane = lax.broadcasted_iota(jnp.int32, (keep_ref.shape[0], LANES), 1)
        traces = jnp.where(lane == 0, full, jnp.where(lane == 1, kept, 0.0))
        low = half_ref[0, 0] == 0
        for out in (keep_ref, send_ref):
            if slot != own:
                out[...] = jnp.zeros_like(out)
            out[:, size:] = traces
        for q in range(devices // 2):
            even = gram_ref[2 * q * own:(2 * q + 1) * own]
            uneven = gram_ref[(2 * q + 1) * own:(2 * q + 2) * own]
            keep_ref[q * slot:q * slot + own, :size] = jnp.where(low, even, uneven)
            send_ref[q * slot:q * slot + own, :size] = jnp.where(low, uneven, even)


def local_gram(chunks, fault, turn, parts, devices, half):
    width = chunks[0].shape[-1]
    each = chunks[0].shape[0] // parts
    noise = fault.shape[2]
    columns = turn.shape[1]
    views = by_part(chunks, parts)
    slot = -(-columns // devices // 8) * 8
    slots = (devices // 2 * slot, columns + LANES)
    out = in_hbm(slots, jnp.float32)
    return pl.pallas_call(
        functools.partial(gram_kernel, len(views), each, devices),
        grid=(3,),
        out_shape=(out, out),
        in_specs=[
            pl.BlockSpec((parts, each, 1, v.shape[3], width), lambda f: (0, 0, f, 0, 0))
            for v in views
        ] + [
            pl.BlockSpec((1, each, noise, width), lambda f: (f, 0, 0, 0)),
            pl.BlockSpec(turn.shape, lambda f: (0, 0)),
            pl.BlockSpec(memory_space=pltpu.SMEM),
        ],
        out_specs=[pl.BlockSpec(slots, lambda f: (0, 0))] * 2,
        scratch_shapes=[pltpu.VMEM((columns, columns), jnp.float32)],
        compiler_params=pltpu.CompilerParams(vmem_limit_bytes=VMEM_BYTES),
        cost_estimate=pl.CostEstimate(
            flops=2 * 3 * each * width * columns * columns,
            bytes_accessed=2 * 3 * each * width * columns,
            transcendentals=0,
        ),
        name="gram",
    )(*views, fault, turn, half)


def add_kernel(count, parts, me_ref, *refs):
    total = refs[0][...]
    for ref in refs[1:count]:
        total = total + ref[...]
    total_ref = refs[-1]
    total_ref[...] = total
    rows = total.shape[0] // parts
    for k in range(parts):
        first = pl.multiple_of(jnp.bitwise_xor(me_ref[0, 0], k) * rows, 8)
        refs[count + k][...] = total_ref[pl.ds(first, rows)]


def add_and_cut(terms, me, parts):
    rows, width = terms[0].shape
    whole = pl.BlockSpec((rows, width), lambda: (0, 0))
    block = pl.BlockSpec((rows // parts, width), lambda: (0, 0))
    return pl.pallas_call(
        functools.partial(add_kernel, len(terms), parts),
        out_shape=[in_hbm((rows // parts, width), jnp.float32) for _ in range(parts)],
        in_specs=[pl.BlockSpec(memory_space=pltpu.SMEM)] + [whole for _ in terms],
        out_specs=[block for _ in range(parts)],
        scratch_shapes=[pltpu.VMEM((rows, width), jnp.float32)],
        compiler_params=pltpu.CompilerParams(vmem_limit_bytes=VMEM_BYTES),
        cost_estimate=pl.CostEstimate(
            flops=len(terms) * rows * width,
            bytes_accessed=4 * (len(terms) + 1) * rows * width,
            transcendentals=0,
        ),
        name="add",
    )(me.reshape(1, 1), *terms)


def partners(axis, distance):
    return [(i, i ^ distance) for i in range(lax.axis_size(axis))]


def sum_over_slabs(keep, send):
    other = lax.ppermute(send, "mode", partners("mode", 1))
    count = lax.axis_size("space")
    blocks = add_and_cut([keep, other], lax.axis_index("space"), count)
    terms = [blocks[0]] + [
        lax.ppermute(blocks[k], "space", partners("space", k)) for k in range(1, count)
    ]
    return add_and_cut(terms, lax.axis_index("mode") // 2, lax.axis_size("mode") // 2)


def sum_over_modes(blocks):
    return blocks[0] + sum(
        lax.ppermute(block, "mode", partners("mode", 2 * k))
        for k, block in enumerate(blocks) if k > 0
    )


def finish_kernel(aliased, scale_ref, swap_ref, x_ref, *refs):
    out_ref = refs[aliased]
    parts, _, each, _, width = x_ref.shape
    rows = parts * each
    scale = scale_ref[0, 0]
    value = x_ref[...].reshape(rows * GROUP, width)
    for top in range(0, rows, GROUP):
        block = value[top * GROUP:(top + GROUP) * GROUP]
        block = scale * jnp.dot(swap_ref[...], block, preferred_element_type=jnp.float32)
        out_ref[:, 0, top:top + GROUP, :] = block.astype(jnp.bfloat16).reshape(GROUP, GROUP, width)


def finish_fields(first, arrived, scale, previous):
    parts, fields, each, modes, width = arrived.shape
    rows = parts * each
    swap = swap_matrix(GROUP, GROUP)
    operands = [scale.reshape(1, 1), swap, arrived, *previous]
    return pl.pallas_call(
        functools.partial(finish_kernel, len(previous)),
        grid=(fields, modes // GROUP),
        out_shape=jax.ShapeDtypeStruct((modes, 3, rows, width), jnp.bfloat16),
        in_specs=[
            pl.BlockSpec(memory_space=pltpu.SMEM),
            pl.BlockSpec(swap.shape, lambda f, m: (0, 0)),
            pl.BlockSpec((parts, 1, each, GROUP, width), lambda f, m: (0, f, 0, m, 0)),
        ] + [pl.BlockSpec(memory_space=pltpu.HBM) for _ in previous],
        out_specs=pl.BlockSpec((GROUP, 1, rows, width), lambda f, m: (m, first + f, 0, 0)),
        input_output_aliases={3: 0} if previous else {},
        compiler_params=pltpu.CompilerParams(vmem_limit_bytes=VMEM_BYTES),
        cost_estimate=pl.CostEstimate(
            flops=fields * modes * rows * width,
            bytes_accessed=4 * fields * modes * rows * width,
            transcendentals=0,
        ),
        name="finish",
    )(*operands)


def send_edges(first, last):
    count = lax.axis_size("space")
    forward = [(i, i + 1) for i in range(count - 1)]
    backward = [(target, source) for source, target in forward]
    return lax.ppermute(last, "space", forward), lax.ppermute(first, "space", backward)


def shards(sqrt_factors, model_error, water_depth, sea_mask, givens_transform):
    modes, fields, rows, width = sqrt_factors.shape
    parts = lax.axis_size("mode")
    count = modes // GROUP
    swap = functools.partial(
        lax.all_to_all, axis_name="mode", split_axis=0, concat_axis=0, tiled=True
    )

    near = min(count, 2)
    water_depth, sea_mask = (
        pltpu.with_memory_space_constraint(value, pltpu.HBM) for value in (water_depth, sea_mask)
    )
    factors = pltpu.with_memory_space_constraint(sqrt_factors, pltpu.HBM)
    head = send_edges(*cut_edges(0, near, factors, (water_depth, sea_mask)))
    cut = cut_edges(near, count - near, factors, ()) if count > near else ()
    *head, = lax.optimization_barrier((*head, *cut))
    head, cut = head[:2], head[2:]
    static = (*head, water_depth, sea_mask)
    near_block = pltpu.with_memory_space_constraint(sqrt_factors[:GROUP], pltpu.VMEM)
    chunks = [swap(forecast_groups(0, 1, 0, 0, 1, (), near_block, *head, *static))]
    rest = ()
    if near > 1:
        rest = (forecast_groups(1, 1, 1, 0, count - 1, rest, sqrt_factors, *head, *static),)
    if count > near:
        tail = send_edges(*cut)
        rest = (forecast_groups(
            near, count - near, 0, near - 1, count - 1, rest, sqrt_factors, *tail, *static
        ),)
    chunks += [swap(value) for value in rest]

    fault = model_error.transpose(1, 2, 0, 3)
    turn = givens_transform.T
    devices = lax.axis_size("space") * parts
    half = lax.rem(lax.axis_index("mode"), 2).reshape(1, 1)
    columns = turn.shape[1]
    cell_count = float(fields * rows * lax.axis_size("space") * width)

    arrived = swap(rotate_fields(0, 2, chunks, fault, turn, parts))
    blocks = sum_over_slabs(*local_gram(chunks, fault, turn, parts, devices, half))
    last = rotate_fields(2, fields - 2, chunks, fault, turn, parts)
    last, total = lax.optimization_barrier((last, sum_over_modes(blocks)))
    last = swap(last)
    gram = total[:columns // devices, :columns] / cell_count
    inflation = jnp.sqrt(total[0, columns] / total[0, columns + 1])

    reduced = finish_fields(0, arrived, inflation, ())
    reduced = finish_fields(2, last, inflation, (reduced,))
    return (reduced, gram, inflation)


def solution(mesh):
    in_specs = (
        P("mode", None, "space", None),
        P(None, None, ("space", "mode"), None),
        P("space", None),
        P("space", None),
        P(),
    )
    out_specs = (P("mode", None, "space", None), P(("space", "mode"), None), P())
    return jax.shard_map(shards, mesh=mesh, in_specs=in_specs, out_specs=out_specs, check_vma=False)
```

profile of v0, /device:TPU:0, one launch (start us, length us, event | category | flops | bytes accessed | tf_op | source)
XLA Modules:
  0.0 280.8 jit_solution(15353541574583669078)
XLA Ops:
  0.6 2.1 cut_edges.2
  2.7 5.0 %collective-permute-start = (bf16[100,4,512]{2,1,0:T(4,128)(2,1)S(1)}, bf16[100,4,512]{2,1,0:T(4,128)(2,1)S(1)}, u32[]{:S(2)}, u32[]{:S(2)}) collective-permute-start(bf16[100,4,512]{2,1,0:T(4,128)(2,1)S(1)} %get-tuple-element.23), channel_id=1, source_target_pairs={{0,8},{8,16},{16,24},{1,9},{9,17},{17,25},{2,10},{10,18},{18,26},{... | collective-permute-start | bytes 1228808 | tf_op jit(solution)/shard_map/ppermute | solution.py:507
  7.7 1.3 collective-permute-start.1
  9.0 2.7 cut_edges.3
  11.7 0.0 copy-start
  11.7 0.0 copy-start.3
  11.7 1.9 slice.12.x_ref
  13.6 2.8 collective-permute-done.low_ref.low_static
  16.3 4.1 %collective-permute-done.1.high_ref.high_static = bf16[100,4,512]{2,1,0:T(4,128)(2,1)S(1)} collective-permute-done((bf16[100,4,512]{2,1,0:T(4,128)(2,1)S(1)}, bf16[100,4,512]{2,1,0:T(4,128)(2,1)S(1)}, u32[]{:S(2)}, u32[]{:S(2)}) %collective-permute-start.1) | collective-permute-done | bytes 409632 | tf_op jit(solution)/shard_map/ppermute | solution.py:507
  20.5 0.0 copy-done
  20.5 0.0 copy-done.3
  20.5 7.2 %forecast.3 = bf16[48,3,16,512]{3,2,1,0:T(8,128)(2,1)} custom-call(bf16[16,3,48,512]{3,2,1,0:T(8,128)(2,1)S(1)} %slice.12.x_ref, bf16[100,4,512]{2,1,0:T(4,128)(2,1)S(1)} %collective-permute-done.low_ref.low_static, bf16[100,4,512]{2,1,0:T(4,128)(2,1)S(1)} %collective-permute-done.1.high_ref.high_static, ...), custom_call_target="tpu_custom_call" | custom-call | flops 23592960 | bytes 4718592 | tf_op jit(solution)/shard_map/forecast/pallas_call | solution.py:242
  27.7 3.7 %all-to-all-start = ((bf16[48,3,16,512]{3,2,1,0:T(8,128)(2,1)}), bf16[48,3,16,512]{3,2,1,0:T(8,128)(2,1)S(1)}, u32[]{:S(2)}, u32[]{:S(2)}) async-start(bf16[48,3,16,512]{3,2,1,0:T(8,128)(2,1)} %forecast.3), calls=%async_computation | async-start | bytes 4718592 | tf_op jit(solution)/shard_map/all_to_all | solution.py:529
  31.5 3.5 %collective-permute-start.2 = (bf16[96,4,512]{2,1,0:T(4,128)(2,1)}, bf16[96,4,512]{2,1,0:T(4,128)(2,1)S(1)}, u32[]{:S(2)}, u32[]{:S(2)}) collective-permute-start(bf16[96,4,512]{2,1,0:T(4,128)(2,1)} %get-tuple-element.29), channel_id=1, source_target_pairs={{0,8},{8,16},{16,24},{1,9},{9,17},{17,25},{2,10},{10,18},{18,26},{... | collective-permute-start | bytes 1179656 | tf_op jit(solution)/shard_map/ppermute | solution.py:507
  34.9 1.5 collective-permute-start.3
  36.4 8.0 %forecast.4.refs_0_ = bf16[48,3,48,512]{3,2,1,0:T(8,128)(2,1)} custom-call(bf16[64,3,48,512]{3,2,1,0:T(8,128)(2,1)} %x_ref.3, bf16[100,4,512]{2,1,0:T(4,128)(2,1)S(1)} %collective-permute-done.low_ref.low_static, bf16[100,4,512]{2,1,0:T(4,128)(2,1)S(1)} %collective-permute-done.1.high_ref.high_static, ...), custom_call_target="tpu_custom_call" | custom-call | flops 23592960 | bytes 4718592 | tf_op jit(solution)/shard_map/forecast/pallas_call | solution.py:242
  44.4 0.0 collective-permute-done.2.low_ref
  44.4 3.8 %collective-permute-done.3.high_ref = bf16[96,4,512]{2,1,0:T(4,128)(2,1)S(1)} collective-permute-done((bf16[96,4,512]{2,1,0:T(4,128)(2,1)}, bf16[96,4,512]{2,1,0:T(4,128)(2,1)S(1)}, u32[]{:S(2)}, u32[]{:S(2)}) %collective-permute-start.3) | collective-permute-done | bytes 393248 | tf_op jit(solution)/shard_map/ppermute | solution.py:507
  48.3 12.9 %forecast.5 = bf16[48,3,48,512]{3,2,1,0:T(8,128)(2,1)} custom-call(bf16[64,3,48,512]{3,2,1,0:T(8,128)(2,1)} %x_ref.3, bf16[96,4,512]{2,1,0:T(4,128)(2,1)S(1)} %collective-permute-done.2.low_ref, bf16[96,4,512]{2,1,0:T(4,128)(2,1)S(1)} %collective-permute-done.3.high_ref, ...), custom_call_target="tpu_custom_call", output_to_operand_aliasing={{}: (9, {})} | custom-call | flops 47185920 | bytes 9437184 | tf_op jit(solution)/shard_map/forecast/pallas_call | solution.py:242
  61.2 0.0 all-to-all-done
  61.2 4.8 %all-to-all-start.1 = ((bf16[48,3,48,512]{3,2,1,0:T(8,128)(2,1)}), bf16[48,3,48,512]{3,2,1,0:T(8,128)(2,1)}, u32[]{:S(2)}, u32[]{:S(2)}) async-start(bf16[48,3,48,512]{3,2,1,0:T(8,128)(2,1)} %forecast.5), calls=%async_computation.1 | async-start | bytes 14155776 | tf_op jit(solution)/shard_map/all_to_all | solution.py:538
  66.0 1.4 copy.18
  67.4 78.6 %all-to-all-done.1 = bf16[48,3,48,512]{3,2,1,0:T(8,128)(2,1)} async-done(((bf16[48,3,48,512]{3,2,1,0:T(8,128)(2,1)}), bf16[48,3,48,512]{3,2,1,0:T(8,128)(2,1)}, u32[]{:S(2)}, u32[]{:S(2)}) %all-to-all-start.1) | async-done | bytes 7077920 | tf_op jit(solution)/shard_map/all_to_all | solution.py:538
  146.0 9.1 %rotate.3 = bf16[8,2,6,64,512]{4,3,2,1,0:T(8,128)(2,1)} custom-call(bf16[8,6,3,16,512]{4,3,2,1,0:T(8,128)(2,1)S(1)} %bitcast.8, bf16[8,6,3,48,512]{4,3,2,1,0:T(8,128)(2,1)} %bitcast.1.refs_1_, bf16[3,6,256,512]{3,2,1,0:T(8,128)(2,1)} %bitcast.14, bf16[512,768]{1,0:T(8,128)(2,1)S(1)} %bitcast.11), custom_call_target="tpu_custom_call" | custom-call | flops 4831838208 | bytes 15728640 | tf_op jit(solution)/shard_map/rotate/pallas_call | solution.py:307
  155.1 5.0 %all-to-all-start.3 = ((bf16[8,2,6,64,512]{4,3,2,1,0:T(8,128)(2,1)}), bf16[8,2,6,64,512]{4,3,2,1,0:T(8,128)(2,1)}, u32[]{:S(2)}, u32[]{:S(2)}) async-start(bf16[8,2,6,64,512]{4,3,2,1,0:T(8,128)(2,1)} %rotate.3), calls=%async_computation.3 | async-start | bytes 12582912 | tf_op jit(solution)/shard_map/all_to_all | solution.py:547
  160.1 18.4 %gram.1 = (f32[384,896]{1,0:T(8,128)}, f32[384,896]{1,0:T(8,128)}) custom-call(bf16[8,6,3,16,512]{4,3,2,1,0:T(8,128)(2,1)S(1)} %bitcast.9, bf16[8,6,3,48,512]{4,3,2,1,0:T(8,128)(2,1)} %bitcast.1.refs_1_, bf16[3,6,256,512]{3,2,1,0:T(8,128)(2,1)} %bitcast.15, bf16[512,768]{1,0:T(8,128)(2,1)S(1)} %bitcast.12, s32[1,1]{1,0:T(1,128)} %bitcast.6.refs_4_), custom_call_target="tpu_custom_call" | custom-call | flops 10871635968 | bytes 14155776 | tf_op jit(solution)/shard_map/gram/pallas_call | solution.py:388
  178.6 0.1 collective-permute-start.4
  178.7 3.3 %collective-permute-done.4.refs_1_ = f32[384,896]{1,0:T(8,128)} collective-permute-done((f32[384,896]{1,0:T(8,128)}, f32[384,896]{1,0:T(8,128)}, u32[]{:S(2)}, u32[]{:S(2)}) %collective-permute-start.4) | collective-permute-done | bytes 1376288 | tf_op jit(solution)/shard_map/ppermute | solution.py:449
  182.0 0.0 copy-start.1
  182.0 1.3 copy-done.1
  183.4 2.6 add.18
  186.0 1.5 collective-permute-start.5
  187.5 0.8 collective-permute-start.6
  188.3 2.0 collective-permute-start.7
  190.4 12.7 %collective-permute-done.5.refs_1_ = f32[96,896]{1,0:T(8,128)} collective-permute-done((f32[96,896]{1,0:T(8,128)}, f32[96,896]{1,0:T(8,128)}, u32[]{:S(2)}, u32[]{:S(2)}) %collective-permute-start.5) | collective-permute-done | bytes 344096 | tf_op jit(solution)/shard_map/ppermute | solution.py:453
  203.1 11.4 %collective-permute-done.6.refs_2_ = f32[96,896]{1,0:T(8,128)} collective-permute-done((f32[96,896]{1,0:T(8,128)}, f32[96,896]{1,0:T(8,128)}, u32[]{:S(2)}, u32[]{:S(2)}) %collective-permute-start.6) | collective-permute-done | bytes 344096 | tf_op jit(solution)/shard_map/ppermute | solution.py:453
  214.4 0.0 collective-permute-done.7.refs_3_
  214.4 0.0 copy-start.2
  214.4 1.0 copy-done.2
  215.4 2.0 add.19
  217.4 1.7 collective-permute-start.8
  219.1 1.5 collective-permute-start.9
  220.6 0.0 copy-start.4
  220.6 0.3 collective-permute-start.10
  220.9 5.5 %rotate.2 = bf16[8,1,6,64,512]{4,3,2,1,0:T(8,128)(2,1)} custom-call(bf16[8,6,3,16,512]{4,3,2,1,0:T(8,128)(2,1)S(1)} %bitcast.10, bf16[8,6,3,48,512]{4,3,2,1,0:T(8,128)(2,1)} %bitcast.1.refs_1_, bf16[3,6,256,512]{3,2,1,0:T(8,128)(2,1)} %bitcast.16, bf16[512,768]{1,0:T(8,128)(2,1)S(1)} %bitcast.13), custom_call_target="tpu_custom_call" | custom-call | flops 2415919104 | bytes 7864320 | tf_op jit(solution)/shard_map/rotate/pallas_call | solution.py:307
  226.4 6.4 %collective-permute-done.8 = f32[24,896]{1,0:T(8,128)S(1)} collective-permute-done((f32[24,896]{1,0:T(8,128)}, f32[24,896]{1,0:T(8,128)S(1)}, u32[]{:S(2)}, u32[]{:S(2)}) %collective-permute-start.8) | collective-permute-done | bytes 86048 | tf_op jit(solution)/shard_map/ppermute | solution.py:460
  232.8 0.8 collective-permute-done.9
  233.7 1.5 collective-permute-done.10
  235.1 0.0 copy-done.4
  235.2 0.0 all-to-all-done.3.x_ref
  235.2 3.7 %all-to-all-start.2 = ((bf16[8,1,6,64,512]{4,3,2,1,0:T(8,128)(2,1)}), bf16[8,1,6,64,512]{4,3,2,1,0:T(8,128)(2,1)S(1)}, u32[]{:S(2)}, u32[]{:S(2)}) async-start(bf16[8,1,6,64,512]{4,3,2,1,0:T(8,128)(2,1)} %rotate.2), calls=%async_computation.2 | async-start | bytes 6291456 | tf_op jit(solution)/shard_map/all_to_all | solution.py:551
  238.8 0.6 fusion
  240.8 0.6 slice_multiply_fusion
  241.4 9.1 %finish.2.refs_0_ = bf16[64,3,48,512]{3,2,1,0:T(8,128)(2,1)} custom-call(f32[1,1]{1,0:T(1,128)} %sqrt.6.scale_ref, bf16[256,256]{1,0:T(8,128)(2,1)S(1)} %copy-done, bf16[8,2,6,64,512]{4,3,2,1,0:T(8,128)(2,1)} %all-to-all-done.3.x_ref), custom_call_target="tpu_custom_call" | custom-call | flops 3145728 | bytes 12582912 | tf_op jit(solution)/shard_map/finish/pallas_call | solution.py:482
  250.5 26.1 %all-to-all-done.2.x_ref = bf16[8,1,6,64,512]{4,3,2,1,0:T(8,128)(2,1)S(1)} async-done(((bf16[8,1,6,64,512]{4,3,2,1,0:T(8,128)(2,1)}), bf16[8,1,6,64,512]{4,3,2,1,0:T(8,128)(2,1)S(1)}, u32[]{:S(2)}, u32[]{:S(2)}) %all-to-all-start.2) | async-done | bytes 3145760 | tf_op jit(solution)/shard_map/all_to_all | solution.py:551
  276.6 3.1 %finish.3 = bf16[64,3,48,512]{3,2,1,0:T(8,128)(2,1)} custom-call(f32[1,1]{1,0:T(1,128)} %sqrt.6.scale_ref, bf16[256,256]{1,0:T(8,128)(2,1)S(1)} %copy-done, bf16[8,1,6,64,512]{4,3,2,1,0:T(8,128)(2,1)S(1)} %all-to-all-done.2.x_ref, bf16[64,3,48,512]{3,2,1,0:T(8,128)(2,1)} %finish.2.refs_0_), custom_call_target="tpu_custom_call", output_to_operand_aliasing={{}: (3, {})} | custom-call | flops 1572864 | bytes 6291456 | tf_op jit(solution)/shard_map/finish/pallas_call | solution.py:482
  (1 shorter events, 0.0 us)
Async XLA Ops:
  2.7 13.6 %collective-permute-start = (bf16[100,4,512]{2,1,0:T(4,128)(2,1)S(1)}, bf16[100,4,512]{2,1,0:T(4,128)(2,1)S(1)}, u32[]{:S(2)}, u32[]{:S(2)}) collective-permute-start(bf16[100,4,512]{2,1,0:T(4,128)(2,1)S(1)} %get-tuple-element.23), channel_id=1, source_target_pairs={{0,8},{8,16},{16,24},{1,9},{9,17},{17,25},{2,10},{10,18},{18,26},{... | collective-permute-start | bytes 1228808 | tf_op jit(solution)/shard_map/ppermute | solution.py:507
  7.7 12.8 %collective-permute-start.1 = (bf16[100,4,512]{2,1,0:T(4,128)(2,1)S(1)}, bf16[100,4,512]{2,1,0:T(4,128)(2,1)S(1)}, u32[]{:S(2)}, u32[]{:S(2)}) collective-permute-start(bf16[100,4,512]{2,1,0:T(4,128)(2,1)S(1)} %get-tuple-element.24), channel_id=1, source_target_pairs={{8,0},{16,8},{24,16},{9,1},{17,9},{25,17},{10,2},{18,10},{26,18},{... | collective-permute-start | bytes 1228808 | tf_op jit(solution)/shard_map/ppermute | solution.py:507
  11.7 8.8 %copy-start = (bf16[256,256]{1,0:T(8,128)(2,1)S(1)}, bf16[256,256]{1,0:T(8,128)(2,1)}, u32[]{:S(2)}) copy-start(bf16[256,256]{1,0:T(8,128)(2,1)} %constant.29.clone.swap_ref) | copy-start | bytes 393220
  11.7 8.8 %copy-start.3 = (bf16[128,128]{1,0:T(8,128)(2,1)S(1)}, bf16[128,128]{1,0:T(8,128)(2,1)}, u32[]{:S(2)}) copy-start(bf16[128,128]{1,0:T(8,128)(2,1)} %constant.30.clone.swap_ends_ref) | copy-start | bytes 98308
  27.7 33.4 %all-to-all-start = ((bf16[48,3,16,512]{3,2,1,0:T(8,128)(2,1)}), bf16[48,3,16,512]{3,2,1,0:T(8,128)(2,1)S(1)}, u32[]{:S(2)}, u32[]{:S(2)}) async-start(bf16[48,3,16,512]{3,2,1,0:T(8,128)(2,1)} %forecast.3), calls=%async_computation | async-start | bytes 4718592 | tf_op jit(solution)/shard_map/all_to_all | solution.py:529
  31.5 13.0 %collective-permute-start.2 = (bf16[96,4,512]{2,1,0:T(4,128)(2,1)}, bf16[96,4,512]{2,1,0:T(4,128)(2,1)S(1)}, u32[]{:S(2)}, u32[]{:S(2)}) collective-permute-start(bf16[96,4,512]{2,1,0:T(4,128)(2,1)} %get-tuple-element.29), channel_id=1, source_target_pairs={{0,8},{8,16},{16,24},{1,9},{9,17},{17,25},{2,10},{10,18},{18,26},{... | collective-permute-start | bytes 1179656 | tf_op jit(solution)/shard_map/ppermute | solution.py:507
  34.9 13.3 %collective-permute-start.3 = (bf16[96,4,512]{2,1,0:T(4,128)(2,1)}, bf16[96,4,512]{2,1,0:T(4,128)(2,1)S(1)}, u32[]{:S(2)}, u32[]{:S(2)}) collective-permute-start(bf16[96,4,512]{2,1,0:T(4,128)(2,1)} %get-tuple-element.30), channel_id=1, source_target_pairs={{8,0},{16,8},{24,16},{9,1},{17,9},{25,17},{10,2},{18,10},{26,18},{... | collective-permute-start | bytes 1179656 | tf_op jit(solution)/shard_map/ppermute | solution.py:507
  61.2 84.9 %all-to-all-start.1 = ((bf16[48,3,48,512]{3,2,1,0:T(8,128)(2,1)}), bf16[48,3,48,512]{3,2,1,0:T(8,128)(2,1)}, u32[]{:S(2)}, u32[]{:S(2)}) async-start(bf16[48,3,48,512]{3,2,1,0:T(8,128)(2,1)} %forecast.5), calls=%async_computation.1 | async-start | bytes 14155776 | tf_op jit(solution)/shard_map/all_to_all | solution.py:538
  155.1 80.0 %all-to-all-start.3 = ((bf16[8,2,6,64,512]{4,3,2,1,0:T(8,128)(2,1)}), bf16[8,2,6,64,512]{4,3,2,1,0:T(8,128)(2,1)}, u32[]{:S(2)}, u32[]{:S(2)}) async-start(bf16[8,2,6,64,512]{4,3,2,1,0:T(8,128)(2,1)} %rotate.3), calls=%async_computation.3 | async-start | bytes 12582912 | tf_op jit(solution)/shard_map/all_to_all | solution.py:547
  178.6 3.5 %collective-permute-start.4 = (f32[384,896]{1,0:T(8,128)}, f32[384,896]{1,0:T(8,128)}, u32[]{:S(2)}, u32[]{:S(2)}) collective-permute-start(f32[384,896]{1,0:T(8,128)} %get-tuple-element.32), channel_id=1, source_target_pairs={{0,1},{1,0},{2,3},{3,2},{4,5},{5,4},{6,7},{7,6},{8,9},{9,8},{10,11... | collective-permute-start | bytes 4128776 | tf_op jit(solution)/shard_map/ppermute | solution.py:449
  182.0 1.3 copy-start.1
  186.0 17.1 %collective-permute-start.5 = (f32[96,896]{1,0:T(8,128)}, f32[96,896]{1,0:T(8,128)}, u32[]{:S(2)}, u32[]{:S(2)}) collective-permute-start(f32[96,896]{1,0:T(8,128)} %get-tuple-element.34), channel_id=1, source_target_pairs={{0,8},{8,0},{16,24},{24,16},{1,9},{9,1},{17,25},{25,17},{2,10},{10... | collective-permute-start | bytes 1032200 | tf_op jit(solution)/shard_map/ppermute | solution.py:453
  187.5 26.9 %collective-permute-start.6 = (f32[96,896]{1,0:T(8,128)}, f32[96,896]{1,0:T(8,128)}, u32[]{:S(2)}, u32[]{:S(2)}) collective-permute-start(f32[96,896]{1,0:T(8,128)} %get-tuple-element.35), channel_id=1, source_target_pairs={{0,16},{8,24},{16,0},{24,8},{1,17},{9,25},{17,1},{25,9},{2,18},{10... | collective-permute-start | bytes 1032200 | tf_op jit(solution)/shard_map/ppermute | solution.py:453
  188.3 26.1 %collective-permute-start.7 = (f32[96,896]{1,0:T(8,128)}, f32[96,896]{1,0:T(8,128)}, u32[]{:S(2)}, u32[]{:S(2)}) collective-permute-start(f32[96,896]{1,0:T(8,128)} %get-tuple-element.36), channel_id=1, source_target_pairs={{0,24},{8,16},{16,8},{24,0},{1,25},{9,17},{17,9},{25,1},{2,26},{10... | collective-permute-start | bytes 1032200 | tf_op jit(solution)/shard_map/ppermute | solution.py:453
  214.4 1.0 copy-start.2
  217.4 15.4 %collective-permute-start.8 = (f32[24,896]{1,0:T(8,128)}, f32[24,896]{1,0:T(8,128)S(1)}, u32[]{:S(2)}, u32[]{:S(2)}) collective-permute-start(f32[24,896]{1,0:T(8,128)} %get-tuple-element.38), channel_id=1, source_target_pairs={{0,2},{1,3},{2,0},{3,1},{4,6},{5,7},{6,4},{7,5},{8,10},{9,11},{10,... | collective-permute-start | bytes 258056 | tf_op jit(solution)/shard_map/ppermute | solution.py:460
  219.1 14.6 %collective-permute-start.9 = (f32[24,896]{1,0:T(8,128)}, f32[24,896]{1,0:T(8,128)S(1)}, u32[]{:S(2)}, u32[]{:S(2)}) collective-permute-start(f32[24,896]{1,0:T(8,128)} %get-tuple-element.39), channel_id=1, source_target_pairs={{0,4},{1,5},{2,6},{3,7},{4,0},{5,1},{6,2},{7,3},{8,12},{9,13},{10,... | collective-permute-start | bytes 258056 | tf_op jit(solution)/shard_map/ppermute | solution.py:460
  220.6 14.5 %copy-start.4 = (f32[24,896]{1,0:T(8,128)S(1)}, f32[24,896]{1,0:T(8,128)}, u32[]{:S(2)}) copy-start(f32[24,896]{1,0:T(8,128)} %get-tuple-element.37) | copy-start | bytes 258052
  220.6 14.5 %collective-permute-start.10 = (f32[24,896]{1,0:T(8,128)}, f32[24,896]{1,0:T(8,128)S(1)}, u32[]{:S(2)}, u32[]{:S(2)}) collective-permute-start(f32[24,896]{1,0:T(8,128)} %get-tuple-element.40), channel_id=1, source_target_pairs={{0,6},{1,7},{2,4},{3,5},{4,2},{5,3},{6,0},{7,1},{8,14},{9,15},{10,... | collective-permute-start | bytes 258056 | tf_op jit(solution)/shard_map/ppermute | solution.py:460
  235.2 41.5 %all-to-all-start.2 = ((bf16[8,1,6,64,512]{4,3,2,1,0:T(8,128)(2,1)}), bf16[8,1,6,64,512]{4,3,2,1,0:T(8,128)(2,1)S(1)}, u32[]{:S(2)}, u32[]{:S(2)}) async-start(bf16[8,1,6,64,512]{4,3,2,1,0:T(8,128)(2,1)} %rotate.2), calls=%async_computation.2 | async-start | bytes 6291456 | tf_op jit(solution)/shard_map/all_to_all | solution.py:551
where the time goes:
time: 282 us; the launch traced here: 281 us
  waiting for transfers between devices  152 us (54%)
  Pallas kernels  82.7 us (29%)
  starting transfers between devices  36.4 us (13%)
  local copies, waits for them, and re-layouts  6.18 us (2%)
  between operations  3.25 us (1%)
    all_to_all x1, waiting for transfers between devices, shards(): chunks += [swap(value) for value in rest]  78.6 us
    pallas_call x3, Pallas kernels, forecast_groups(): pl.pallas_call(forecast_kernel, grid=(count,), out_shape=in_hbm((rows, fi...  28.1 us
    all_to_all x1, waiting for transfers between devices, shards(): last = swap(last)  26.1 us
    ppermute x3, waiting for transfers between devices, sum_over_slabs(): lax.ppermute(blocks[k], 'space', partners('space', k))  24.1 us
    pallas_call x1, Pallas kernels, local_gram(): pl.pallas_call(functools.partial(gram_kernel, len(views), each, devices),...  18.4 us
    pallas_call x2, Pallas kernels, rotate_fields(): pl.pallas_call(functools.partial(rotate_kernel, len(views)), grid=(fields...  14.6 us
    pallas_call x2, Pallas kernels, finish_fields(): pl.pallas_call(functools.partial(finish_kernel, len(previous)), grid=(fie...  12.2 us
    ppermute x3, waiting for transfers between devices, sum_over_modes(): lax.ppermute(block, 'mode', partners('mode', 2 * k))  8.71 us
  transfers between devices with their start and end apart: 15, of which 11 were waited for; matrix products, arithmetic and copies ran while one was open for 2% of the time, Pallas kernels for 22%

commit v1 on v0

--- a/solution.py
+++ b/solution.py
@@ -95,43 +95,9 @@
     return max(size for size in range(1, 55) if count % size == 0)
 
 
-def forecast_kernel(x_ref, low_ref, high_ref, low_static, high_static, depth_ref, mask_ref,
-                    swap_ref, swap_ends_ref, *refs):
-    out_ref, cells, ends, depth, wet, surf1, east1, north1, surf2 = refs[-9:]
-    _, fields, rows, width = x_ref.shape
+def two_steps(rows, width, cells, depth, wet, surf1, east1, north1, surf2, put_row):
     tiles = width // LANES
     spots = [slice(t * LANES, (t + 1) * LANES) for t in range(tiles)]
-
-    ends[:, :HALO] = low_ref[...].astype(jnp.float32)
-    ends[:, HALO:] = high_ref[...].astype(jnp.float32)
-    for field in range(fields):
-        for top in range(0, rows, GROUP):
-            block = x_ref[:, field, top:top + GROUP, :].reshape(GROUP * GROUP, width)
-            block = jnp.dot(swap_ref[...], block, preferred_element_type=jnp.float32)
-            block = block * slope_coef if field == 0 else block
-            cells[field, HALO + top:HALO + top + GROUP] = block.reshape(GROUP, GROUP, width)
-        block = jnp.concatenate([ends[m * fields + field] for m in range(GROUP)], axis=0)
-        block = jnp.dot(
-            swap_ends_ref[...], block.astype(jnp.bfloat16), preferred_element_type=jnp.float32
-        ).reshape(2 * HALO, GROUP, width)
-        block = block * slope_coef if field == 0 else block
-        cells[field, :HALO] = block[:HALO]
-        cells[field, HALO + rows:] = block[HALO:]
-
-    def place_static(place, depth_row, wet_row):
-        depth[place] = jnp.broadcast_to(flux_coef * slope_coef * depth_row, (8, width))
-        wet[place] = jnp.broadcast_to(wet_row, (8, width))
-
-    for static, first in ((low_static, 0), (high_static, HALO + rows)):
-        value = static[...].astype(jnp.float32)
-        level = value[0] + value[1] + value[2]
-        for j in range(HALO):
-            place_static(first + j, level[j:j + 1], value[3, j:j + 1])
-    for top in range(0, rows, 8):
-        level = depth_ref[top:top + 8]
-        sea = mask_ref[top:top + 8].astype(jnp.float32)
-        for j in range(8):
-            place_static(HALO + top + j, level[j:j + 1], sea[j:j + 1])
 
     def get(ref, i):
         return [ref[i, :, spot] for spot in spots]
@@ -212,7 +178,7 @@
             surface = [value * (1.0 / slope_coef) for value in surface]
             for field, values in enumerate((surface, east, north)):
                 for spot, value in zip(spots, values):
-                    out_ref[r, field, :, spot] = value.astype(jnp.bfloat16)
+                    put_row(r, field, spot, value.astype(jnp.bfloat16))
 
         flows(
             i, size, lambda r: get(surf2, r + 1), lambda r: get(east1, r + 2),
@@ -223,6 +189,192 @@
     over_rows(-2, rows + 2, first_flow)
     over_rows(-1, rows + 1, second_surface)
     over_rows(0, rows, second_flow)
+
+
+def place_static(depth, wet, first, levels, seas):
+    for j in range(levels.shape[0]):
+        shape = depth.shape[1:]
+        depth[first + j] = jnp.broadcast_to(flux_coef * slope_coef * levels[j:j + 1], shape)
+        wet[first + j] = jnp.broadcast_to(seas[j:j + 1], shape)
+
+
+def place_message_static(depth, wet, first, static_ref):
+    value = static_ref[...].astype(jnp.float32)
+    place_static(depth, wet, first, value[0] + value[1] + value[2], value[3])
+
+
+def place_own_static(depth, wet, first, depth_ref, mask_ref, low, count):
+    for top in range(low, low + count, 8):
+        place_static(depth, wet, first + top - low, depth_ref[top:top + 8],
+                     mask_ref[top:top + 8].astype(jnp.float32))
+
+
+def spread_rows(x, swap_ref, field):
+    width = x.shape[-1]
+    block = jnp.dot(swap_ref[...], x.reshape(GROUP * GROUP, width), preferred_element_type=jnp.float32)
+    block = block * slope_coef if field == 0 else block
+    return block.reshape(GROUP, GROUP, width)
+
+
+def spread_edges(ends, low_ref, high_ref, swap_ends_ref, field, fields):
+    width = low_ref.shape[-1]
+    if field == 0:
+        ends[:, :HALO] = low_ref[...].astype(jnp.float32)
+        ends[:, HALO:] = high_ref[...].astype(jnp.float32)
+    block = jnp.concatenate([ends[m * fields + field] for m in range(GROUP)], axis=0)
+    block = jnp.dot(
+        swap_ends_ref[...], block.astype(jnp.bfloat16), preferred_element_type=jnp.float32
+    ).reshape(2 * HALO, GROUP, width)
+    return block * slope_coef if field == 0 else block
+
+
+def forecast_kernel(x_ref, low_ref, high_ref, low_static, high_static, depth_ref, mask_ref,
+                    swap_ref, swap_ends_ref, *refs):
+    out_ref, cells, ends, depth, wet = refs[-9:-4]
+    _, fields, rows, width = x_ref.shape
+
+    for field in range(fields):
+        for top in range(0, rows, GROUP):
+            cells[field, HALO + top:HALO + top + GROUP] = spread_rows(
+                x_ref[:, field, top:top + GROUP, :], swap_ref, field
+            )
+        block = spread_edges(ends, low_ref, high_ref, swap_ends_ref, field, fields)
+        cells[field, :HALO] = block[:HALO]
+        cells[field, HALO + rows:] = block[HALO:]
+    place_message_static(depth, wet, 0, low_static)
+    place_message_static(depth, wet, HALO + rows, high_static)
+    place_own_static(depth, wet, HALO, depth_ref, mask_ref, 0, rows)
+
+    def put_row(r, field, spot, value):
+        out_ref[r, field, :, spot] = value
+
+    two_steps(rows, width, cells, depth, wet, *refs[-4:], put_row)
+
+
+def inner_kernel(x_ref, depth_ref, mask_ref, swap_ref, out_ref, cells, depth, wet, *steps):
+    _, fields, rows, width = x_ref.shape
+    for field in range(fields):
+        for top in range(0, rows, GROUP):
+            cells[field, HALO + top:HALO + top + GROUP] = spread_rows(
+                x_ref[:, field, top:top + GROUP, :], swap_ref, field
+            )
+    for ref in (depth, wet, *(cells.at[field] for field in range(fields))):
+        ref[:HALO] = jnp.zeros((HALO,) + ref.shape[1:], jnp.float32)
+        ref[HALO + rows:] = jnp.zeros((HALO,) + ref.shape[1:], jnp.float32)
+    place_own_static(depth, wet, HALO, depth_ref, mask_ref, 0, rows)
+
+    def put_row(r, field, spot, value):
+        out_ref[r, field, :, spot] = value
+
+    two_steps(rows, width, cells, depth, wet, *steps, put_row)
+
+
+def outer_kernel(first_ref, last_ref, low_ref, high_ref, low_static, high_static, depth_ref,
+                 mask_ref, swap_ref, swap_ends_ref, inner_ref, out_ref,
+                 cells, ends, edge, depth, wet, surf1, east1, north1, surf2, turned, sems):
+    _, fields, _, width = first_ref.shape
+    rows = out_ref.shape[0]
+    for field in range(fields):
+        edge[field] = spread_edges(ends, low_ref, high_ref, swap_ends_ref, field, fields)
+    copies = []
+    for side, (x_ref, first) in enumerate(((first_ref, 0), (last_ref, rows - HALO))):
+        for field in range(fields):
+            block = spread_rows(x_ref[:, field], swap_ref, field)
+            if side == 0:
+                cells[field, :HALO] = edge[field, :HALO]
+                cells[field, HALO:] = block[:2 * HALO]
+            else:
+                cells[field, :2 * HALO] = block[GROUP - 2 * HALO:]
+                cells[field, 2 * HALO:] = edge[field, HALO:]
+        if side == 0:
+            place_message_static(depth, wet, 0, low_static)
+            place_own_static(depth, wet, HALO, depth_ref, mask_ref, 0, 2 * HALO)
+        else:
+            place_own_static(depth, wet, 0, depth_ref, mask_ref, rows - 2 * HALO, 2 * HALO)
+            place_message_static(depth, wet, 2 * HALO, high_static)
+
+        def put_row(r, field, spot, value):
+            turned[side, r, field, :, spot] = value
+
+        two_steps(HALO, width, cells, depth, wet, surf1, east1, north1, surf2, put_row)
+        copies.append(pltpu.make_async_copy(
+            turned.at[side], out_ref.at[pl.ds(first, HALO)], sems.at[side]
+        ))
+        copies[-1].start()
+    for copy in copies:
+        copy.wait()
+
+
+def step_scratch(rows, width):
+    return [pltpu.VMEM((rows + more, GROUP, width), jnp.float32) for more in (6, 4, 4, 2)]
+
+
+def forecast_inner(factors, depth, mask):
+    _, fields, rows, width = factors.shape
+    padded = rows + 2 * HALO
+    swap = swap_matrix(GROUP, GROUP)
+    return pl.pallas_call(
+        inner_kernel,
+        grid=(1,),
+        out_shape=in_hbm((rows, fields, GROUP, width), jnp.bfloat16),
+        in_specs=[pl.BlockSpec((GROUP, fields, rows, width), lambda i: (0, 0, 0, 0))] + [
+            pl.BlockSpec(value.shape, lambda i: (0, 0)) for value in (depth, mask, swap)
+        ],
+        out_specs=pl.BlockSpec((rows, fields, GROUP, width), lambda i: (0, 0, 0, 0)),
+        scratch_shapes=[
+            pltpu.VMEM((fields, padded, GROUP, width), jnp.float32),
+            pltpu.VMEM((padded, 8, width), jnp.float32),
+            pltpu.VMEM((padded, 8, width), jnp.float32),
+        ] + step_scratch(rows, width),
+        compiler_params=pltpu.CompilerParams(vmem_limit_bytes=VMEM_BYTES),
+        cost_estimate=pl.CostEstimate(
+            flops=60 * GROUP * rows * width,
+            bytes_accessed=2 * 2 * GROUP * fields * rows * width,
+            transcendentals=0,
+        ),
+        name="inner",
+    )(factors, depth, mask, swap)
+
+
+def forecast_outer(inner, factors, low, high, depth, mask):
+    _, fields, rows, width = factors.shape
+    edge = GROUP * fields
+    last = low.shape[0] // 4 - 1
+    swap, swap_ends = swap_matrix(GROUP, GROUP), swap_matrix(2 * HALO, GROUP)
+    return pl.pallas_call(
+        outer_kernel,
+        grid=(1,),
+        out_shape=in_hbm(inner.shape, inner.dtype),
+        in_specs=[
+            pl.BlockSpec((GROUP, fields, GROUP, width), lambda i: (0, 0, 0, 0)),
+            pl.BlockSpec((GROUP, fields, GROUP, width), lambda i: (0, 0, rows // GROUP - 1, 0)),
+            pl.BlockSpec((edge, HALO, width), lambda i: (0, 0, 0)),
+            pl.BlockSpec((edge, HALO, width), lambda i: (0, 0, 0)),
+            pl.BlockSpec((4, HALO, width), lambda i: (last, 0, 0)),
+            pl.BlockSpec((4, HALO, width), lambda i: (last, 0, 0)),
+        ] + [
+            pl.BlockSpec(value.shape, lambda i: (0, 0)) for value in (depth, mask, swap, swap_ends)
+        ] + [pl.BlockSpec(memory_space=pltpu.HBM)],
+        out_specs=pl.BlockSpec(memory_space=pltpu.HBM),
+        input_output_aliases={10: 0},
+        scratch_shapes=[
+            pltpu.VMEM((fields, 3 * HALO, GROUP, width), jnp.float32),
+            pltpu.VMEM((edge, 2 * HALO, width), jnp.float32),
+            pltpu.VMEM((fields, 2 * HALO, GROUP, width), jnp.float32),
+            pltpu.VMEM((3 * HALO, 8, width), jnp.float32),
+            pltpu.VMEM((3 * HALO, 8, width), jnp.float32),
+        ] + step_scratch(HALO, width) + [
+            pltpu.VMEM((2, HALO, fields, GROUP, width), jnp.bfloat16),
+            pltpu.SemaphoreType.DMA((2,)),
+        ],
+        compiler_params=pltpu.CompilerParams(vmem_limit_bytes=VMEM_BYTES),
+        cost_estimate=pl.CostEstimate(
+            flops=20 * GROUP * rows * width,
+            bytes_accessed=2 * 2 * GROUP * fields * GROUP * width,
+            transcendentals=0,
+        ),
+        name="outer",
+    )(factors, factors, low, high, low, high, depth, mask, swap, swap_ends, inner)
 
 
 def forecast_groups(first, count, skip, place, whole_count, previous, factors, low, high,
@@ -232,9 +384,6 @@
     edge = GROUP * fields
     last = static_low.shape[0] // 4 - 1
     swap, swap_ends = swap_matrix(GROUP, GROUP), swap_matrix(2 * HALO, GROUP)
-
-    def rows_of(count):
-        return pltpu.VMEM((count, GROUP, width), jnp.float32)
 
     def whole(value):
         return pl.BlockSpec(value.shape, lambda i: (0,) * value.ndim)
@@ -261,11 +410,7 @@
             pltpu.VMEM((edge, 2 * HALO, width), jnp.float32),
             pltpu.VMEM((padded, 8, width), jnp.float32),
             pltpu.VMEM((padded, 8, width), jnp.float32),
-            rows_of(rows + 6),
-            rows_of(rows + 4),
-            rows_of(rows + 4),
-            rows_of(rows + 2),
-        ],
+        ] + step_scratch(rows, width),
         compiler_params=pltpu.CompilerParams(vmem_limit_bytes=VMEM_BYTES),
         cost_estimate=pl.CostEstimate(
             flops=60 * count * GROUP * rows * width,
@@ -525,8 +670,8 @@
     *head, = lax.optimization_barrier((*head, *cut))
     head, cut = head[:2], head[2:]
     static = (*head, water_depth, sea_mask)
-    near_block = pltpu.with_memory_space_constraint(sqrt_factors[:GROUP], pltpu.VMEM)
-    chunks = [swap(forecast_groups(0, 1, 0, 0, 1, (), near_block, *head, *static))]
+    inner = forecast_inner(sqrt_factors, water_depth, sea_mask)
+    chunks = [swap(forecast_outer(inner, sqrt_factors, *static))]
     rest = ()
     if near > 1:
         rest = (forecast_groups(1, 1, 1, 0, count - 1, rest, sqrt_factors, *head, *static),)

time: 282 us -> 278 us (0.986)
  waiting for transfers between devices: 152 us -> 146 us
  Pallas kernels: 82.7 us -> 86.7 us
    pallas_call x0 -> x2, Pallas kernels: none -> 11.2 us  [the longest x1 7.64 us: forecast_inner(): pl.pallas_call(inner_kernel, grid=(1,), out_shape=in_hbm((rows, fields, G...]
    pallas_call x3 -> x2, Pallas kernels: 28.1 us -> 20.9 us  [forecast_groups(): pl.pallas_call(forecast_kernel, grid=(count,), out_shape=in_hbm((rows, fi...]
    ppermute x2, waiting for transfers between devices: 7.98 us -> 4.99 us  [send_edges(): lax.ppermute(first, 'space', backward)]
  transfers between devices with their start and end apart: 15 -> 15, of which waited for: 11 -> 10; matrix products, arithmetic and copies ran while one was open for 2% -> 1% of each run, Pallas kernels for 22% -> 25%
where the time goes in v1:
time: 278 us; the launch traced here: 277 us
  waiting for transfers between devices  146 us (53%)
  Pallas kernels  86.7 us (31%)
  starting transfers between devices  36.5 us (13%)
  local copies, waits for them, and re-layouts  4.32 us (2%)
  between operations  3.26 us (1%)
    all_to_all x1, waiting for transfers between devices, shards(): chunks += [swap(value) for value in rest]  78.6 us
    all_to_all x1, waiting for transfers between devices, shards(): last = swap(last)  26.1 us
    ppermute x3, waiting for transfers between devices, sum_over_slabs(): lax.ppermute(blocks[k], 'space', partners('space', k))  24.1 us
    pallas_call x2, Pallas kernels, forecast_groups(): pl.pallas_call(forecast_kernel, grid=(count,), out_shape=in_hbm((rows, fi...  20.9 us
    pallas_call x1, Pallas kernels, local_gram(): pl.pallas_call(functools.partial(gram_kernel, len(views), each, devices),...  18.4 us
    pallas_call x2, Pallas kernels, rotate_fields(): pl.pallas_call(functools.partial(rotate_kernel, len(views)), grid=(fields...  14.6 us
    pallas_call x2, Pallas kernels, finish_fields(): pl.pallas_call(functools.partial(finish_kernel, len(previous)), grid=(fie...  12.2 us
    ppermute x3, waiting for transfers between devices, sum_over_modes(): lax.ppermute(block, 'mode', partners('mode', 2 * k))  8.69 us
  transfers between devices with their start and end apart: 15, of which 10 were waited for; matrix products, arithmetic and copies ran while one was open for 1% of the time, Pallas kernels for 25%

profile of v1, /device:TPU:0, one launch (start us, length us, event | category | flops | bytes accessed | tf_op | source)
XLA Modules:
  0.0 277.3 jit_solution(14090935065878895354)
XLA Ops:
  0.6 2.1 cut_edges.2
  2.7 5.0 %collective-permute-start = (bf16[100,4,512]{2,1,0:T(4,128)(2,1)S(1)}, bf16[100,4,512]{2,1,0:T(4,128)(2,1)S(1)}, u32[]{:S(2)}, u32[]{:S(2)}) collective-permute-start(bf16[100,4,512]{2,1,0:T(4,128)(2,1)S(1)} %get-tuple-element.23), channel_id=1, source_target_pairs={{0,8},{8,16},{16,24},{1,9},{9,17},{17,25},{2,10},{10,18},{18,26},{... | collective-permute-start | bytes 1228808 | tf_op jit(solution)/shard_map/ppermute | solution.py:652
  7.7 0.0 copy-start
  7.7 1.4 collective-permute-start.1
  9.1 2.7 cut_edges.3
  11.8 0.0 copy-done
  11.8 0.0 copy-start.3
  11.8 7.6 %inner.1.inner_ref = bf16[48,3,16,512]{3,2,1,0:T(8,128)(2,1)} custom-call(bf16[64,3,48,512]{3,2,1,0:T(8,128)(2,1)} %x_ref.5, f32[48,512]{1,0:T(8,128)} %depth_ref.7, s32[48,512]{1,0:T(8,128)} %mask_ref.7, bf16[256,256]{1,0:T(8,128)(2,1)S(1)} %copy-done), custom_call_target="tpu_custom_call" | custom-call | flops 23592960 | bytes 4718592 | tf_op jit(solution)/shard_map/inner/pallas_call | solution.py:316
  19.5 0.0 collective-permute-done.low_ref.low_static
  19.5 1.1 collective-permute-done.1.high_ref.high_static
  20.6 0.0 copy-done.3
  20.6 3.6 %outer.1 = bf16[48,3,16,512]{3,2,1,0:T(8,128)(2,1)} custom-call(bf16[64,3,48,512]{3,2,1,0:T(8,128)(2,1)} %x_ref.5, bf16[64,3,48,512]{3,2,1,0:T(8,128)(2,1)} %x_ref.5, bf16[100,4,512]{2,1,0:T(4,128)(2,1)S(1)} %collective-permute-done.low_ref.low_static, ...), custom_call_target="tpu_custom_call", output_to_operand_aliasing={{}: (10, {})} | custom-call | flops 7864320 | bytes 1572864 | tf_op jit(solution)/shard_map/outer/pallas_call | solution.py:344
  24.2 3.7 %all-to-all-start = ((bf16[48,3,16,512]{3,2,1,0:T(8,128)(2,1)}), bf16[48,3,16,512]{3,2,1,0:T(8,128)(2,1)S(1)}, u32[]{:S(2)}, u32[]{:S(2)}) async-start(bf16[48,3,16,512]{3,2,1,0:T(8,128)(2,1)} %outer.1), calls=%async_computation | async-start | bytes 4718592 | tf_op jit(solution)/shard_map/all_to_all | solution.py:674
  28.0 3.5 %collective-permute-start.2 = (bf16[96,4,512]{2,1,0:T(4,128)(2,1)}, bf16[96,4,512]{2,1,0:T(4,128)(2,1)S(1)}, u32[]{:S(2)}, u32[]{:S(2)}) collective-permute-start(bf16[96,4,512]{2,1,0:T(4,128)(2,1)} %get-tuple-element.29), channel_id=1, source_target_pairs={{0,8},{8,16},{16,24},{1,9},{9,17},{17,25},{2,10},{10,18},{18,26},{... | collective-permute-start | bytes 1179656 | tf_op jit(solution)/shard_map/ppermute | solution.py:652
  31.4 1.5 collective-permute-start.3
  32.9 8.0 %forecast.2.refs_0_ = bf16[48,3,48,512]{3,2,1,0:T(8,128)(2,1)} custom-call(bf16[64,3,48,512]{3,2,1,0:T(8,128)(2,1)} %x_ref.5, bf16[100,4,512]{2,1,0:T(4,128)(2,1)S(1)} %collective-permute-done.low_ref.low_static, bf16[100,4,512]{2,1,0:T(4,128)(2,1)S(1)} %collective-permute-done.1.high_ref.high_static, ...), custom_call_target="tpu_custom_call" | custom-call | flops 23592960 | bytes 4718592 | tf_op jit(solution)/shard_map/forecast/pallas_call | solution.py:391
  40.9 0.0 collective-permute-done.2.low_ref
  40.9 3.8 %collective-permute-done.3.high_ref = bf16[96,4,512]{2,1,0:T(4,128)(2,1)S(1)} collective-permute-done((bf16[96,4,512]{2,1,0:T(4,128)(2,1)}, bf16[96,4,512]{2,1,0:T(4,128)(2,1)S(1)}, u32[]{:S(2)}, u32[]{:S(2)}) %collective-permute-start.3) | collective-permute-done | bytes 393248 | tf_op jit(solution)/shard_map/ppermute | solution.py:652
  44.8 12.9 %forecast.3 = bf16[48,3,48,512]{3,2,1,0:T(8,128)(2,1)} custom-call(bf16[64,3,48,512]{3,2,1,0:T(8,128)(2,1)} %x_ref.5, bf16[96,4,512]{2,1,0:T(4,128)(2,1)S(1)} %collective-permute-done.2.low_ref, bf16[96,4,512]{2,1,0:T(4,128)(2,1)S(1)} %collective-permute-done.3.high_ref, ...), custom_call_target="tpu_custom_call", output_to_operand_aliasing={{}: (9, {})} | custom-call | flops 47185920 | bytes 9437184 | tf_op jit(solution)/shard_map/forecast/pallas_call | solution.py:391
  57.6 0.0 all-to-all-done
  57.6 4.8 %all-to-all-start.1 = ((bf16[48,3,48,512]{3,2,1,0:T(8,128)(2,1)}), bf16[48,3,48,512]{3,2,1,0:T(8,128)(2,1)}, u32[]{:S(2)}, u32[]{:S(2)}) async-start(bf16[48,3,48,512]{3,2,1,0:T(8,128)(2,1)} %forecast.3), calls=%async_computation.1 | async-start | bytes 14155776 | tf_op jit(solution)/shard_map/all_to_all | solution.py:683
  62.5 1.4 copy.20
  63.9 78.6 %all-to-all-done.1 = bf16[48,3,48,512]{3,2,1,0:T(8,128)(2,1)} async-done(((bf16[48,3,48,512]{3,2,1,0:T(8,128)(2,1)}), bf16[48,3,48,512]{3,2,1,0:T(8,128)(2,1)}, u32[]{:S(2)}, u32[]{:S(2)}) %all-to-all-start.1) | async-done | bytes 7077920 | tf_op jit(solution)/shard_map/all_to_all | solution.py:683
  142.5 9.1 %rotate.3 = bf16[8,2,6,64,512]{4,3,2,1,0:T(8,128)(2,1)} custom-call(bf16[8,6,3,16,512]{4,3,2,1,0:T(8,128)(2,1)S(1)} %bitcast.8, bf16[8,6,3,48,512]{4,3,2,1,0:T(8,128)(2,1)} %bitcast.1.refs_1_, bf16[3,6,256,512]{3,2,1,0:T(8,128)(2,1)} %bitcast.14, bf16[512,768]{1,0:T(8,128)(2,1)S(1)} %bitcast.11), custom_call_target="tpu_custom_call" | custom-call | flops 4831838208 | bytes 15728640 | tf_op jit(solution)/shard_map/rotate/pallas_call | solution.py:452
  151.6 5.0 %all-to-all-start.3 = ((bf16[8,2,6,64,512]{4,3,2,1,0:T(8,128)(2,1)}), bf16[8,2,6,64,512]{4,3,2,1,0:T(8,128)(2,1)}, u32[]{:S(2)}, u32[]{:S(2)}) async-start(bf16[8,2,6,64,512]{4,3,2,1,0:T(8,128)(2,1)} %rotate.3), calls=%async_computation.3 | async-start | bytes 12582912 | tf_op jit(solution)/shard_map/all_to_all | solution.py:692
  156.6 18.4 %gram.1 = (f32[384,896]{1,0:T(8,128)}, f32[384,896]{1,0:T(8,128)}) custom-call(bf16[8,6,3,16,512]{4,3,2,1,0:T(8,128)(2,1)S(1)} %bitcast.9, bf16[8,6,3,48,512]{4,3,2,1,0:T(8,128)(2,1)} %bitcast.1.refs_1_, bf16[3,6,256,512]{3,2,1,0:T(8,128)(2,1)} %bitcast.15, bf16[512,768]{1,0:T(8,128)(2,1)S(1)} %bitcast.12, s32[1,1]{1,0:T(1,128)} %bitcast.6.refs_4_), custom_call_target="tpu_custom_call" | custom-call | flops 10871635968 | bytes 14155776 | tf_op jit(solution)/shard_map/gram/pallas_call | solution.py:533
  175.1 0.1 collective-permute-start.4
  175.2 3.3 %collective-permute-done.4.refs_1_ = f32[384,896]{1,0:T(8,128)} collective-permute-done((f32[384,896]{1,0:T(8,128)}, f32[384,896]{1,0:T(8,128)}, u32[]{:S(2)}, u32[]{:S(2)}) %collective-permute-start.4) | collective-permute-done | bytes 1376288 | tf_op jit(solution)/shard_map/ppermute | solution.py:594
  178.5 0.0 copy-start.1
  178.5 1.3 copy-done.1
  179.9 2.6 add.18
  182.5 1.6 collective-permute-start.5
  184.0 2.3 collective-permute-start.6
  186.3 0.5 collective-permute-start.7
  186.9 12.8 %collective-permute-done.5.refs_1_ = f32[96,896]{1,0:T(8,128)} collective-permute-done((f32[96,896]{1,0:T(8,128)}, f32[96,896]{1,0:T(8,128)}, u32[]{:S(2)}, u32[]{:S(2)}) %collective-permute-start.5) | collective-permute-done | bytes 344096 | tf_op jit(solution)/shard_map/ppermute | solution.py:598
  199.6 11.3 %collective-permute-done.6.refs_2_ = f32[96,896]{1,0:T(8,128)} collective-permute-done((f32[96,896]{1,0:T(8,128)}, f32[96,896]{1,0:T(8,128)}, u32[]{:S(2)}, u32[]{:S(2)}) %collective-permute-start.6) | collective-permute-done | bytes 344096 | tf_op jit(solution)/shard_map/ppermute | solution.py:598
  210.9 0.0 collective-permute-done.7.refs_3_
  210.9 0.0 copy-start.2
  210.9 1.0 copy-done.2
  211.9 2.0 add.19
  213.9 1.7 collective-permute-start.8
  215.6 1.5 collective-permute-start.9
  217.1 0.0 copy-start.4
  217.1 0.3 collective-permute-start.10
  217.4 5.5 %rotate.2 = bf16[8,1,6,64,512]{4,3,2,1,0:T(8,128)(2,1)} custom-call(bf16[8,6,3,16,512]{4,3,2,1,0:T(8,128)(2,1)S(1)} %bitcast.10, bf16[8,6,3,48,512]{4,3,2,1,0:T(8,128)(2,1)} %bitcast.1.refs_1_, bf16[3,6,256,512]{3,2,1,0:T(8,128)(2,1)} %bitcast.16, bf16[512,768]{1,0:T(8,128)(2,1)S(1)} %bitcast.13), custom_call_target="tpu_custom_call" | custom-call | flops 2415919104 | bytes 7864320 | tf_op jit(solution)/shard_map/rotate/pallas_call | solution.py:452
  222.9 6.4 %collective-permute-done.8 = f32[24,896]{1,0:T(8,128)S(1)} collective-permute-done((f32[24,896]{1,0:T(8,128)}, f32[24,896]{1,0:T(8,128)S(1)}, u32[]{:S(2)}, u32[]{:S(2)}) %collective-permute-start.8) | collective-permute-done | bytes 86048 | tf_op jit(solution)/shard_map/ppermute | solution.py:605
  229.3 0.8 collective-permute-done.9
  230.2 1.5 collective-permute-done.10
  231.6 0.0 copy-done.4
  231.6 0.0 all-to-all-done.3.x_ref
  231.7 3.7 %all-to-all-start.2 = ((bf16[8,1,6,64,512]{4,3,2,1,0:T(8,128)(2,1)}), bf16[8,1,6,64,512]{4,3,2,1,0:T(8,128)(2,1)S(1)}, u32[]{:S(2)}, u32[]{:S(2)}) async-start(bf16[8,1,6,64,512]{4,3,2,1,0:T(8,128)(2,1)} %rotate.2), calls=%async_computation.2 | async-start | bytes 6291456 | tf_op jit(solution)/shard_map/all_to_all | solution.py:696
  235.3 0.6 fusion
  237.3 0.6 slice_multiply_fusion
  237.9 9.1 %finish.2.refs_0_ = bf16[64,3,48,512]{3,2,1,0:T(8,128)(2,1)} custom-call(f32[1,1]{1,0:T(1,128)} %sqrt.6.scale_ref, bf16[256,256]{1,0:T(8,128)(2,1)S(1)} %copy-done, bf16[8,2,6,64,512]{4,3,2,1,0:T(8,128)(2,1)} %all-to-all-done.3.x_ref), custom_call_target="tpu_custom_call" | custom-call | flops 3145728 | bytes 12582912 | tf_op jit(solution)/shard_map/finish/pallas_call | solution.py:627
  247.0 26.1 %all-to-all-done.2.x_ref = bf16[8,1,6,64,512]{4,3,2,1,0:T(8,128)(2,1)S(1)} async-done(((bf16[8,1,6,64,512]{4,3,2,1,0:T(8,128)(2,1)}), bf16[8,1,6,64,512]{4,3,2,1,0:T(8,128)(2,1)S(1)}, u32[]{:S(2)}, u32[]{:S(2)}) %all-to-all-start.2) | async-done | bytes 3145760 | tf_op jit(solution)/shard_map/all_to_all | solution.py:696
  273.1 3.1 %finish.3 = bf16[64,3,48,512]{3,2,1,0:T(8,128)(2,1)} custom-call(f32[1,1]{1,0:T(1,128)} %sqrt.6.scale_ref, bf16[256,256]{1,0:T(8,128)(2,1)S(1)} %copy-done, bf16[8,1,6,64,512]{4,3,2,1,0:T(8,128)(2,1)S(1)} %all-to-all-done.2.x_ref, bf16[64,3,48,512]{3,2,1,0:T(8,128)(2,1)} %finish.2.refs_0_), custom_call_target="tpu_custom_call", output_to_operand_aliasing={{}: (3, {})} | custom-call | flops 1572864 | bytes 6291456 | tf_op jit(solution)/shard_map/finish/pallas_call | solution.py:627
  (1 shorter events, 0.0 us)
Async XLA Ops:
  2.7 16.8 %collective-permute-start = (bf16[100,4,512]{2,1,0:T(4,128)(2,1)S(1)}, bf16[100,4,512]{2,1,0:T(4,128)(2,1)S(1)}, u32[]{:S(2)}, u32[]{:S(2)}) collective-permute-start(bf16[100,4,512]{2,1,0:T(4,128)(2,1)S(1)} %get-tuple-element.23), channel_id=1, source_target_pairs={{0,8},{8,16},{16,24},{1,9},{9,17},{17,25},{2,10},{10,18},{18,26},{... | collective-permute-start | bytes 1228808 | tf_op jit(solution)/shard_map/ppermute | solution.py:652
  7.7 4.2 %copy-start = (bf16[256,256]{1,0:T(8,128)(2,1)S(1)}, bf16[256,256]{1,0:T(8,128)(2,1)}, u32[]{:S(2)}) copy-start(bf16[256,256]{1,0:T(8,128)(2,1)} %constant.29.clone.swap_ref) | copy-start | bytes 393220
  7.7 13.0 %collective-permute-start.1 = (bf16[100,4,512]{2,1,0:T(4,128)(2,1)S(1)}, bf16[100,4,512]{2,1,0:T(4,128)(2,1)S(1)}, u32[]{:S(2)}, u32[]{:S(2)}) collective-permute-start(bf16[100,4,512]{2,1,0:T(4,128)(2,1)S(1)} %get-tuple-element.24), channel_id=1, source_target_pairs={{8,0},{16,8},{24,16},{9,1},{17,9},{25,17},{10,2},{18,10},{26,18},{... | collective-permute-start | bytes 1228808 | tf_op jit(solution)/shard_map/ppermute | solution.py:652
  11.8 8.8 %copy-start.3 = (bf16[128,128]{1,0:T(8,128)(2,1)S(1)}, bf16[128,128]{1,0:T(8,128)(2,1)}, u32[]{:S(2)}) copy-start(bf16[128,128]{1,0:T(8,128)(2,1)} %constant.30.clone.swap_ends_ref) | copy-start | bytes 98308
  24.2 33.4 %all-to-all-start = ((bf16[48,3,16,512]{3,2,1,0:T(8,128)(2,1)}), bf16[48,3,16,512]{3,2,1,0:T(8,128)(2,1)S(1)}, u32[]{:S(2)}, u32[]{:S(2)}) async-start(bf16[48,3,16,512]{3,2,1,0:T(8,128)(2,1)} %outer.1), calls=%async_computation | async-start | bytes 4718592 | tf_op jit(solution)/shard_map/all_to_all | solution.py:674
  28.0 13.0 %collective-permute-start.2 = (bf16[96,4,512]{2,1,0:T(4,128)(2,1)}, bf16[96,4,512]{2,1,0:T(4,128)(2,1)S(1)}, u32[]{:S(2)}, u32[]{:S(2)}) collective-permute-start(bf16[96,4,512]{2,1,0:T(4,128)(2,1)} %get-tuple-element.29), channel_id=1, source_target_pairs={{0,8},{8,16},{16,24},{1,9},{9,17},{17,25},{2,10},{10,18},{18,26},{... | collective-permute-start | bytes 1179656 | tf_op jit(solution)/shard_map/ppermute | solution.py:652
  31.4 13.3 %collective-permute-start.3 = (bf16[96,4,512]{2,1,0:T(4,128)(2,1)}, bf16[96,4,512]{2,1,0:T(4,128)(2,1)S(1)}, u32[]{:S(2)}, u32[]{:S(2)}) collective-permute-start(bf16[96,4,512]{2,1,0:T(4,128)(2,1)} %get-tuple-element.30), channel_id=1, source_target_pairs={{8,0},{16,8},{24,16},{9,1},{17,9},{25,17},{10,2},{18,10},{26,18},{... | collective-permute-start | bytes 1179656 | tf_op jit(solution)/shard_map/ppermute | solution.py:652
  57.6 84.9 %all-to-all-start.1 = ((bf16[48,3,48,512]{3,2,1,0:T(8,128)(2,1)}), bf16[48,3,48,512]{3,2,1,0:T(8,128)(2,1)}, u32[]{:S(2)}, u32[]{:S(2)}) async-start(bf16[48,3,48,512]{3,2,1,0:T(8,128)(2,1)} %forecast.3), calls=%async_computation.1 | async-start | bytes 14155776 | tf_op jit(solution)/shard_map/all_to_all | solution.py:683
  151.6 80.0 %all-to-all-start.3 = ((bf16[8,2,6,64,512]{4,3,2,1,0:T(8,128)(2,1)}), bf16[8,2,6,64,512]{4,3,2,1,0:T(8,128)(2,1)}, u32[]{:S(2)}, u32[]{:S(2)}) async-start(bf16[8,2,6,64,512]{4,3,2,1,0:T(8,128)(2,1)} %rotate.3), calls=%async_computation.3 | async-start | bytes 12582912 | tf_op jit(solution)/shard_map/all_to_all | solution.py:692
  175.1 3.5 %collective-permute-start.4 = (f32[384,896]{1,0:T(8,128)}, f32[384,896]{1,0:T(8,128)}, u32[]{:S(2)}, u32[]{:S(2)}) collective-permute-start(f32[384,896]{1,0:T(8,128)} %get-tuple-element.32), channel_id=1, source_target_pairs={{0,1},{1,0},{2,3},{3,2},{4,5},{5,4},{6,7},{7,6},{8,9},{9,8},{10,11... | collective-permute-start | bytes 4128776 | tf_op jit(solution)/shard_map/ppermute | solution.py:594
  178.5 1.3 copy-start.1
  182.5 17.2 %collective-permute-start.5 = (f32[96,896]{1,0:T(8,128)}, f32[96,896]{1,0:T(8,128)}, u32[]{:S(2)}, u32[]{:S(2)}) collective-permute-start(f32[96,896]{1,0:T(8,128)} %get-tuple-element.34), channel_id=1, source_target_pairs={{0,8},{8,0},{16,24},{24,16},{1,9},{9,1},{17,25},{25,17},{2,10},{10... | collective-permute-start | bytes 1032200 | tf_op jit(solution)/shard_map/ppermute | solution.py:598
  184.0 26.9 %collective-permute-start.6 = (f32[96,896]{1,0:T(8,128)}, f32[96,896]{1,0:T(8,128)}, u32[]{:S(2)}, u32[]{:S(2)}) collective-permute-start(f32[96,896]{1,0:T(8,128)} %get-tuple-element.35), channel_id=1, source_target_pairs={{0,16},{8,24},{16,0},{24,8},{1,17},{9,25},{17,1},{25,9},{2,18},{10... | collective-permute-start | bytes 1032200 | tf_op jit(solution)/shard_map/ppermute | solution.py:598
  186.3 24.6 %collective-permute-start.7 = (f32[96,896]{1,0:T(8,128)}, f32[96,896]{1,0:T(8,128)}, u32[]{:S(2)}, u32[]{:S(2)}) collective-permute-start(f32[96,896]{1,0:T(8,128)} %get-tuple-element.36), channel_id=1, source_target_pairs={{0,24},{8,16},{16,8},{24,0},{1,25},{9,17},{17,9},{25,1},{2,26},{10... | collective-permute-start | bytes 1032200 | tf_op jit(solution)/shard_map/ppermute | solution.py:598
  210.9 1.0 copy-start.2
  213.9 15.4 %collective-permute-start.8 = (f32[24,896]{1,0:T(8,128)}, f32[24,896]{1,0:T(8,128)S(1)}, u32[]{:S(2)}, u32[]{:S(2)}) collective-permute-start(f32[24,896]{1,0:T(8,128)} %get-tuple-element.38), channel_id=1, source_target_pairs={{0,2},{1,3},{2,0},{3,1},{4,6},{5,7},{6,4},{7,5},{8,10},{9,11},{10,... | collective-permute-start | bytes 258056 | tf_op jit(solution)/shard_map/ppermute | solution.py:605
  215.6 14.5 %collective-permute-start.9 = (f32[24,896]{1,0:T(8,128)}, f32[24,896]{1,0:T(8,128)S(1)}, u32[]{:S(2)}, u32[]{:S(2)}) collective-permute-start(f32[24,896]{1,0:T(8,128)} %get-tuple-element.39), channel_id=1, source_target_pairs={{0,4},{1,5},{2,6},{3,7},{4,0},{5,1},{6,2},{7,3},{8,12},{9,13},{10,... | collective-permute-start | bytes 258056 | tf_op jit(solution)/shard_map/ppermute | solution.py:605
  217.1 14.5 %copy-start.4 = (f32[24,896]{1,0:T(8,128)S(1)}, f32[24,896]{1,0:T(8,128)}, u32[]{:S(2)}) copy-start(f32[24,896]{1,0:T(8,128)} %get-tuple-element.37) | copy-start | bytes 258052
  217.1 14.5 %collective-permute-start.10 = (f32[24,896]{1,0:T(8,128)}, f32[24,896]{1,0:T(8,128)S(1)}, u32[]{:S(2)}, u32[]{:S(2)}) collective-permute-start(f32[24,896]{1,0:T(8,128)} %get-tuple-element.40), channel_id=1, source_target_pairs={{0,6},{1,7},{2,4},{3,5},{4,2},{5,3},{6,0},{7,1},{8,14},{9,15},{10,... | collective-permute-start | bytes 258056 | tf_op jit(solution)/shard_map/ppermute | solution.py:605
  231.7 41.5 %all-to-all-start.2 = ((bf16[8,1,6,64,512]{4,3,2,1,0:T(8,128)(2,1)}), bf16[8,1,6,64,512]{4,3,2,1,0:T(8,128)(2,1)S(1)}, u32[]{:S(2)}, u32[]{:S(2)}) async-start(bf16[8,1,6,64,512]{4,3,2,1,0:T(8,128)(2,1)} %rotate.2), calls=%async_computation.2 | async-start | bytes 6291456 | tf_op jit(solution)/shard_map/all_to_all | solution.py:696

commit v2 on v1

--- a/solution.py
+++ b/solution.py
@@ -427,12 +427,15 @@
     return joined.reshape(-1, joined.shape[-1]), fault_ref[0, j]
 
 
-def rotate_kernel(count, *refs):
-    chunk_refs = refs[:count]
+def rotate_kernel(count, first, *refs):
+    near_ref, *chunk_refs = refs[:count]
     fault_ref, turn_ref, out_ref = refs[count:]
     parts, _, size, modes, width = out_ref.shape
+    field, top = first + pl.program_id(0), pl.program_id(1) * size
     for j in range(size):
-        columns = jnp.concatenate(all_columns(chunk_refs, fault_ref, j), axis=0)
+        own = [near_ref[:, top + j, field]] + [ref[:, j, 0] for ref in chunk_refs]
+        prior = jnp.concatenate(own, axis=1).reshape(-1, width)
+        columns = jnp.concatenate([prior, fault_ref[0, j]], axis=0)
         value = jnp.dot(turn_ref[...], columns, preferred_element_type=jnp.float32)
         out_ref[:, 0, j] = value.astype(jnp.bfloat16).reshape(parts, modes, width)
 
@@ -450,15 +453,15 @@
     size = 3 if each % 3 == 0 else 1
     views = by_part(chunks, parts)
     return pl.pallas_call(
-        functools.partial(rotate_kernel, len(views)),
+        functools.partial(rotate_kernel, len(views), first),
         grid=(fields, each // size),
         out_shape=in_hbm((parts, fields, each, modes, width), jnp.bfloat16),
-        in_specs=[
+        in_specs=[pl.BlockSpec(memory_space=pltpu.VMEM)] + [
             pl.BlockSpec((parts, size, 1, v.shape[3], width), lambda f, j: (0, j, first + f, 0, 0))
-            for v in views
+            for v in views[1:]
         ] + [
             pl.BlockSpec((1, size, noise, width), lambda f, j: (first + f, j, 0, 0)),
-            pl.BlockSpec(turn.shape, lambda f, j: (0, 0)),
+            pl.BlockSpec(memory_space=pltpu.VMEM),
         ],
         out_specs=pl.BlockSpec((parts, 1, size, modes, width), lambda f, j: (0, f, j, 0, 0)),
         compiler_params=pltpu.CompilerParams(vmem_limit_bytes=VMEM_BYTES),

time: 278 us -> 278 us (level)
  no operation moved by 1% of the time
where the time goes in v2:
time: 278 us; the launch traced here: 277 us
  waiting for transfers between devices  146 us (53%)
  Pallas kernels  86.6 us (31%)
  starting transfers between devices  36.5 us (13%)
  local copies, waits for them, and re-layouts  4.32 us (2%)
  between operations  3.26 us (1%)
    all_to_all x1, waiting for transfers between devices, shards(): chunks += [swap(value) for value in rest]  78.6 us
    all_to_all x1, waiting for transfers between devices, shards(): last = swap(last)  26.1 us
    ppermute x3, waiting for transfers between devices, sum_over_slabs(): lax.ppermute(blocks[k], 'space', partners('space', k))  24.1 us
    pallas_call x2, Pallas kernels, forecast_groups(): pl.pallas_call(forecast_kernel, grid=(count,), out_shape=in_hbm((rows, fi...  20.9 us
    pallas_call x1, Pallas kernels, local_gram(): pl.pallas_call(functools.partial(gram_kernel, len(views), each, devices),...  18.4 us
    pallas_call x2, Pallas kernels, rotate_fields(): pl.pallas_call(functools.partial(rotate_kernel, len(views), first), grid=...  14.5 us
    pallas_call x2, Pallas kernels, finish_fields(): pl.pallas_call(functools.partial(finish_kernel, len(previous)), grid=(fie...  12.2 us
    ppermute x3, waiting for transfers between devices, sum_over_modes(): lax.ppermute(block, 'mode', partners('mode', 2 * k))  8.72 us
  transfers between devices with their start and end apart: 15, of which 10 were waited for; matrix products, arithmetic and copies ran while one was open for 1% of the time, Pallas kernels for 25%

profile of v2, /device:TPU:0, one launch (start us, length us, event | category | flops | bytes accessed | tf_op | source)
XLA Modules:
  0.0 277.3 jit_solution(5100915395189551987)
XLA Ops:
  0.6 2.1 cut_edges.2
  2.7 5.0 %collective-permute-start = (bf16[100,4,512]{2,1,0:T(4,128)(2,1)S(1)}, bf16[100,4,512]{2,1,0:T(4,128)(2,1)S(1)}, u32[]{:S(2)}, u32[]{:S(2)}) collective-permute-start(bf16[100,4,512]{2,1,0:T(4,128)(2,1)S(1)} %get-tuple-element.23), channel_id=1, source_target_pairs={{0,8},{8,16},{16,24},{1,9},{9,17},{17,25},{2,10},{10,18},{18,26},{... | collective-permute-start | bytes 1228808 | tf_op jit(solution)/shard_map/ppermute | solution.py:655
  7.7 0.0 copy-start
  7.7 1.4 collective-permute-start.1
  9.1 2.7 cut_edges.3
  11.8 0.0 copy-done
  11.8 0.0 copy-start.3
  11.8 7.6 %inner.1.inner_ref = bf16[48,3,16,512]{3,2,1,0:T(8,128)(2,1)} custom-call(bf16[64,3,48,512]{3,2,1,0:T(8,128)(2,1)} %x_ref.5, f32[48,512]{1,0:T(8,128)} %depth_ref.7, s32[48,512]{1,0:T(8,128)} %mask_ref.7, bf16[256,256]{1,0:T(8,128)(2,1)S(1)} %copy-done), custom_call_target="tpu_custom_call" | custom-call | flops 23592960 | bytes 4718592 | tf_op jit(solution)/shard_map/inner/pallas_call | solution.py:316
  19.5 0.0 collective-permute-done.low_ref.low_static
  19.5 1.1 collective-permute-done.1.high_ref.high_static
  20.6 0.0 copy-done.3
  20.6 3.6 %outer.1 = bf16[48,3,16,512]{3,2,1,0:T(8,128)(2,1)} custom-call(bf16[64,3,48,512]{3,2,1,0:T(8,128)(2,1)} %x_ref.5, bf16[64,3,48,512]{3,2,1,0:T(8,128)(2,1)} %x_ref.5, bf16[100,4,512]{2,1,0:T(4,128)(2,1)S(1)} %collective-permute-done.low_ref.low_static, ...), custom_call_target="tpu_custom_call", output_to_operand_aliasing={{}: (10, {})} | custom-call | flops 7864320 | bytes 1572864 | tf_op jit(solution)/shard_map/outer/pallas_call | solution.py:344
  24.2 3.7 %all-to-all-start = ((bf16[48,3,16,512]{3,2,1,0:T(8,128)(2,1)}), bf16[48,3,16,512]{3,2,1,0:T(8,128)(2,1)S(1)}, u32[]{:S(2)}, u32[]{:S(2)}) async-start(bf16[48,3,16,512]{3,2,1,0:T(8,128)(2,1)} %outer.1), calls=%async_computation | async-start | bytes 4718592 | tf_op jit(solution)/shard_map/all_to_all | solution.py:677
  28.0 3.5 %collective-permute-start.2 = (bf16[96,4,512]{2,1,0:T(4,128)(2,1)}, bf16[96,4,512]{2,1,0:T(4,128)(2,1)S(1)}, u32[]{:S(2)}, u32[]{:S(2)}) collective-permute-start(bf16[96,4,512]{2,1,0:T(4,128)(2,1)} %get-tuple-element.29), channel_id=1, source_target_pairs={{0,8},{8,16},{16,24},{1,9},{9,17},{17,25},{2,10},{10,18},{18,26},{... | collective-permute-start | bytes 1179656 | tf_op jit(solution)/shard_map/ppermute | solution.py:655
  31.4 1.5 collective-permute-start.3
  32.9 8.0 %forecast.2.refs_0_ = bf16[48,3,48,512]{3,2,1,0:T(8,128)(2,1)} custom-call(bf16[64,3,48,512]{3,2,1,0:T(8,128)(2,1)} %x_ref.5, bf16[100,4,512]{2,1,0:T(4,128)(2,1)S(1)} %collective-permute-done.low_ref.low_static, bf16[100,4,512]{2,1,0:T(4,128)(2,1)S(1)} %collective-permute-done.1.high_ref.high_static, ...), custom_call_target="tpu_custom_call" | custom-call | flops 23592960 | bytes 4718592 | tf_op jit(solution)/shard_map/forecast/pallas_call | solution.py:391
  40.9 0.0 collective-permute-done.2.low_ref
  40.9 3.8 %collective-permute-done.3.high_ref = bf16[96,4,512]{2,1,0:T(4,128)(2,1)S(1)} collective-permute-done((bf16[96,4,512]{2,1,0:T(4,128)(2,1)}, bf16[96,4,512]{2,1,0:T(4,128)(2,1)S(1)}, u32[]{:S(2)}, u32[]{:S(2)}) %collective-permute-start.3) | collective-permute-done | bytes 393248 | tf_op jit(solution)/shard_map/ppermute | solution.py:655
  44.8 12.9 %forecast.3 = bf16[48,3,48,512]{3,2,1,0:T(8,128)(2,1)} custom-call(bf16[64,3,48,512]{3,2,1,0:T(8,128)(2,1)} %x_ref.5, bf16[96,4,512]{2,1,0:T(4,128)(2,1)S(1)} %collective-permute-done.2.low_ref, bf16[96,4,512]{2,1,0:T(4,128)(2,1)S(1)} %collective-permute-done.3.high_ref, ...), custom_call_target="tpu_custom_call", output_to_operand_aliasing={{}: (9, {})} | custom-call | flops 47185920 | bytes 9437184 | tf_op jit(solution)/shard_map/forecast/pallas_call | solution.py:391
  57.6 0.0 all-to-all-done
  57.6 4.8 %all-to-all-start.1 = ((bf16[48,3,48,512]{3,2,1,0:T(8,128)(2,1)}), bf16[48,3,48,512]{3,2,1,0:T(8,128)(2,1)}, u32[]{:S(2)}, u32[]{:S(2)}) async-start(bf16[48,3,48,512]{3,2,1,0:T(8,128)(2,1)} %forecast.3), calls=%async_computation.1 | async-start | bytes 14155776 | tf_op jit(solution)/shard_map/all_to_all | solution.py:686
  62.5 1.4 copy.20
  63.9 78.6 %all-to-all-done.1 = bf16[48,3,48,512]{3,2,1,0:T(8,128)(2,1)} async-done(((bf16[48,3,48,512]{3,2,1,0:T(8,128)(2,1)}), bf16[48,3,48,512]{3,2,1,0:T(8,128)(2,1)}, u32[]{:S(2)}, u32[]{:S(2)}) %all-to-all-start.1) | async-done | bytes 7077920 | tf_op jit(solution)/shard_map/all_to_all | solution.py:686
  142.5 9.1 %rotate.3 = bf16[8,2,6,64,512]{4,3,2,1,0:T(8,128)(2,1)} custom-call(bf16[8,6,3,16,512]{4,3,2,1,0:T(8,128)(2,1)S(1)} %bitcast.8, bf16[8,6,3,48,512]{4,3,2,1,0:T(8,128)(2,1)} %bitcast.1.refs_1_, bf16[3,6,256,512]{3,2,1,0:T(8,128)(2,1)} %bitcast.14, bf16[512,768]{1,0:T(8,128)(2,1)S(1)} %bitcast.11), custom_call_target="tpu_custom_call" | custom-call | flops 4831838208 | bytes 15728640 | tf_op jit(solution)/shard_map/rotate/pallas_call | solution.py:455
  151.6 5.0 %all-to-all-start.3 = ((bf16[8,2,6,64,512]{4,3,2,1,0:T(8,128)(2,1)}), bf16[8,2,6,64,512]{4,3,2,1,0:T(8,128)(2,1)}, u32[]{:S(2)}, u32[]{:S(2)}) async-start(bf16[8,2,6,64,512]{4,3,2,1,0:T(8,128)(2,1)} %rotate.3), calls=%async_computation.3 | async-start | bytes 12582912 | tf_op jit(solution)/shard_map/all_to_all | solution.py:695
  156.6 18.4 %gram.1 = (f32[384,896]{1,0:T(8,128)}, f32[384,896]{1,0:T(8,128)}) custom-call(bf16[8,6,3,16,512]{4,3,2,1,0:T(8,128)(2,1)S(1)} %bitcast.9, bf16[8,6,3,48,512]{4,3,2,1,0:T(8,128)(2,1)} %bitcast.1.refs_1_, bf16[3,6,256,512]{3,2,1,0:T(8,128)(2,1)} %bitcast.15, bf16[512,768]{1,0:T(8,128)(2,1)S(1)} %bitcast.12, s32[1,1]{1,0:T(1,128)} %bitcast.6.refs_4_), custom_call_target="tpu_custom_call" | custom-call | flops 10871635968 | bytes 14155776 | tf_op jit(solution)/shard_map/gram/pallas_call | solution.py:536
  175.0 0.1 collective-permute-start.4
  175.1 3.3 %collective-permute-done.4.refs_1_ = f32[384,896]{1,0:T(8,128)} collective-permute-done((f32[384,896]{1,0:T(8,128)}, f32[384,896]{1,0:T(8,128)}, u32[]{:S(2)}, u32[]{:S(2)}) %collective-permute-start.4) | collective-permute-done | bytes 1376288 | tf_op jit(solution)/shard_map/ppermute | solution.py:597
  178.5 0.0 copy-start.1
  178.5 1.3 copy-done.1
  179.8 2.6 add.18
  182.4 1.6 collective-permute-start.5
  184.0 2.3 collective-permute-start.6
  186.3 0.5 collective-permute-start.7
  186.8 12.8 %collective-permute-done.5.refs_1_ = f32[96,896]{1,0:T(8,128)} collective-permute-done((f32[96,896]{1,0:T(8,128)}, f32[96,896]{1,0:T(8,128)}, u32[]{:S(2)}, u32[]{:S(2)}) %collective-permute-start.5) | collective-permute-done | bytes 344096 | tf_op jit(solution)/shard_map/ppermute | solution.py:601
  199.6 11.3 %collective-permute-done.6.refs_2_ = f32[96,896]{1,0:T(8,128)} collective-permute-done((f32[96,896]{1,0:T(8,128)}, f32[96,896]{1,0:T(8,128)}, u32[]{:S(2)}, u32[]{:S(2)}) %collective-permute-start.6) | collective-permute-done | bytes 344096 | tf_op jit(solution)/shard_map/ppermute | solution.py:601
  210.9 0.0 collective-permute-done.7.refs_3_
  210.9 0.0 copy-start.2
  210.9 1.0 copy-done.2
  211.9 2.0 add.19
  213.9 1.7 collective-permute-start.8
  215.6 1.5 collective-permute-start.9
  217.0 0.0 copy-start.4
  217.0 0.3 collective-permute-start.10
  217.4 5.5 %rotate.2 = bf16[8,1,6,64,512]{4,3,2,1,0:T(8,128)(2,1)} custom-call(bf16[8,6,3,16,512]{4,3,2,1,0:T(8,128)(2,1)S(1)} %bitcast.10, bf16[8,6,3,48,512]{4,3,2,1,0:T(8,128)(2,1)} %bitcast.1.refs_1_, bf16[3,6,256,512]{3,2,1,0:T(8,128)(2,1)} %bitcast.16, bf16[512,768]{1,0:T(8,128)(2,1)S(1)} %bitcast.13), custom_call_target="tpu_custom_call" | custom-call | flops 2415919104 | bytes 7864320 | tf_op jit(solution)/shard_map/rotate/pallas_call | solution.py:455
  222.8 6.4 %collective-permute-done.8 = f32[24,896]{1,0:T(8,128)S(1)} collective-permute-done((f32[24,896]{1,0:T(8,128)}, f32[24,896]{1,0:T(8,128)S(1)}, u32[]{:S(2)}, u32[]{:S(2)}) %collective-permute-start.8) | collective-permute-done | bytes 86048 | tf_op jit(solution)/shard_map/ppermute | solution.py:608
  229.3 0.8 collective-permute-done.9
  230.1 1.5 collective-permute-done.10
  231.6 0.0 copy-done.4
  231.6 0.0 all-to-all-done.3.x_ref
  231.6 3.7 %all-to-all-start.2 = ((bf16[8,1,6,64,512]{4,3,2,1,0:T(8,128)(2,1)}), bf16[8,1,6,64,512]{4,3,2,1,0:T(8,128)(2,1)S(1)}, u32[]{:S(2)}, u32[]{:S(2)}) async-start(bf16[8,1,6,64,512]{4,3,2,1,0:T(8,128)(2,1)} %rotate.2), calls=%async_computation.2 | async-start | bytes 6291456 | tf_op jit(solution)/shard_map/all_to_all | solution.py:699
  235.3 0.6 fusion
  237.2 0.6 slice_multiply_fusion
  237.9 9.1 %finish.2.refs_0_ = bf16[64,3,48,512]{3,2,1,0:T(8,128)(2,1)} custom-call(f32[1,1]{1,0:T(1,128)} %sqrt.6.scale_ref, bf16[256,256]{1,0:T(8,128)(2,1)S(1)} %copy-done, bf16[8,2,6,64,512]{4,3,2,1,0:T(8,128)(2,1)} %all-to-all-done.3.x_ref), custom_call_target="tpu_custom_call" | custom-call | flops 3145728 | bytes 12582912 | tf_op jit(solution)/shard_map/finish/pallas_call | solution.py:630
  247.0 26.1 %all-to-all-done.2.x_ref = bf16[8,1,6,64,512]{4,3,2,1,0:T(8,128)(2,1)S(1)} async-done(((bf16[8,1,6,64,512]{4,3,2,1,0:T(8,128)(2,1)}), bf16[8,1,6,64,512]{4,3,2,1,0:T(8,128)(2,1)S(1)}, u32[]{:S(2)}, u32[]{:S(2)}) %all-to-all-start.2) | async-done | bytes 3145760 | tf_op jit(solution)/shard_map/all_to_all | solution.py:699
  273.1 3.1 %finish.3 = bf16[64,3,48,512]{3,2,1,0:T(8,128)(2,1)} custom-call(f32[1,1]{1,0:T(1,128)} %sqrt.6.scale_ref, bf16[256,256]{1,0:T(8,128)(2,1)S(1)} %copy-done, bf16[8,1,6,64,512]{4,3,2,1,0:T(8,128)(2,1)S(1)} %all-to-all-done.2.x_ref, bf16[64,3,48,512]{3,2,1,0:T(8,128)(2,1)} %finish.2.refs_0_), custom_call_target="tpu_custom_call", output_to_operand_aliasing={{}: (3, {})} | custom-call | flops 1572864 | bytes 6291456 | tf_op jit(solution)/shard_map/finish/pallas_call | solution.py:630
  (1 shorter events, 0.0 us)
Async XLA Ops:
  2.7 16.8 %collective-permute-start = (bf16[100,4,512]{2,1,0:T(4,128)(2,1)S(1)}, bf16[100,4,512]{2,1,0:T(4,128)(2,1)S(1)}, u32[]{:S(2)}, u32[]{:S(2)}) collective-permute-start(bf16[100,4,512]{2,1,0:T(4,128)(2,1)S(1)} %get-tuple-element.23), channel_id=1, source_target_pairs={{0,8},{8,16},{16,24},{1,9},{9,17},{17,25},{2,10},{10,18},{18,26},{... | collective-permute-start | bytes 1228808 | tf_op jit(solution)/shard_map/ppermute | solution.py:655
  7.7 4.2 %copy-start = (bf16[256,256]{1,0:T(8,128)(2,1)S(1)}, bf16[256,256]{1,0:T(8,128)(2,1)}, u32[]{:S(2)}) copy-start(bf16[256,256]{1,0:T(8,128)(2,1)} %constant.29.clone.swap_ref) | copy-start | bytes 393220
  7.7 13.0 %collective-permute-start.1 = (bf16[100,4,512]{2,1,0:T(4,128)(2,1)S(1)}, bf16[100,4,512]{2,1,0:T(4,128)(2,1)S(1)}, u32[]{:S(2)}, u32[]{:S(2)}) collective-permute-start(bf16[100,4,512]{2,1,0:T(4,128)(2,1)S(1)} %get-tuple-element.24), channel_id=1, source_target_pairs={{8,0},{16,8},{24,16},{9,1},{17,9},{25,17},{10,2},{18,10},{26,18},{... | collective-permute-start | bytes 1228808 | tf_op jit(solution)/shard_map/ppermute | solution.py:655
  11.8 8.8 %copy-start.3 = (bf16[128,128]{1,0:T(8,128)(2,1)S(1)}, bf16[128,128]{1,0:T(8,128)(2,1)}, u32[]{:S(2)}) copy-start(bf16[128,128]{1,0:T(8,128)(2,1)} %constant.30.clone.swap_ends_ref) | copy-start | bytes 98308
  24.2 33.4 %all-to-all-start = ((bf16[48,3,16,512]{3,2,1,0:T(8,128)(2,1)}), bf16[48,3,16,512]{3,2,1,0:T(8,128)(2,1)S(1)}, u32[]{:S(2)}, u32[]{:S(2)}) async-start(bf16[48,3,16,512]{3,2,1,0:T(8,128)(2,1)} %outer.1), calls=%async_computation | async-start | bytes 4718592 | tf_op jit(solution)/shard_map/all_to_all | solution.py:677
  28.0 13.0 %collective-permute-start.2 = (bf16[96,4,512]{2,1,0:T(4,128)(2,1)}, bf16[96,4,512]{2,1,0:T(4,128)(2,1)S(1)}, u32[]{:S(2)}, u32[]{:S(2)}) collective-permute-start(bf16[96,4,512]{2,1,0:T(4,128)(2,1)} %get-tuple-element.29), channel_id=1, source_target_pairs={{0,8},{8,16},{16,24},{1,9},{9,17},{17,25},{2,10},{10,18},{18,26},{... | collective-permute-start | bytes 1179656 | tf_op jit(solution)/shard_map/ppermute | solution.py:655
  31.4 13.3 %collective-permute-start.3 = (bf16[96,4,512]{2,1,0:T(4,128)(2,1)}, bf16[96,4,512]{2,1,0:T(4,128)(2,1)S(1)}, u32[]{:S(2)}, u32[]{:S(2)}) collective-permute-start(bf16[96,4,512]{2,1,0:T(4,128)(2,1)} %get-tuple-element.30), channel_id=1, source_target_pairs={{8,0},{16,8},{24,16},{9,1},{17,9},{25,17},{10,2},{18,10},{26,18},{... | collective-permute-start | bytes 1179656 | tf_op jit(solution)/shard_map/ppermute | solution.py:655
  57.6 84.9 %all-to-all-start.1 = ((bf16[48,3,48,512]{3,2,1,0:T(8,128)(2,1)}), bf16[48,3,48,512]{3,2,1,0:T(8,128)(2,1)}, u32[]{:S(2)}, u32[]{:S(2)}) async-start(bf16[48,3,48,512]{3,2,1,0:T(8,128)(2,1)} %forecast.3), calls=%async_computation.1 | async-start | bytes 14155776 | tf_op jit(solution)/shard_map/all_to_all | solution.py:686
  151.6 80.0 %all-to-all-start.3 = ((bf16[8,2,6,64,512]{4,3,2,1,0:T(8,128)(2,1)}), bf16[8,2,6,64,512]{4,3,2,1,0:T(8,128)(2,1)}, u32[]{:S(2)}, u32[]{:S(2)}) async-start(bf16[8,2,6,64,512]{4,3,2,1,0:T(8,128)(2,1)} %rotate.3), calls=%async_computation.3 | async-start | bytes 12582912 | tf_op jit(solution)/shard_map/all_to_all | solution.py:695
  175.0 3.5 %collective-permute-start.4 = (f32[384,896]{1,0:T(8,128)}, f32[384,896]{1,0:T(8,128)}, u32[]{:S(2)}, u32[]{:S(2)}) collective-permute-start(f32[384,896]{1,0:T(8,128)} %get-tuple-element.32), channel_id=1, source_target_pairs={{0,1},{1,0},{2,3},{3,2},{4,5},{5,4},{6,7},{7,6},{8,9},{9,8},{10,11... | collective-permute-start | bytes 4128776 | tf_op jit(solution)/shard_map/ppermute | solution.py:597
  178.5 1.3 copy-start.1
  182.4 17.2 %collective-permute-start.5 = (f32[96,896]{1,0:T(8,128)}, f32[96,896]{1,0:T(8,128)}, u32[]{:S(2)}, u32[]{:S(2)}) collective-permute-start(f32[96,896]{1,0:T(8,128)} %get-tuple-element.34), channel_id=1, source_target_pairs={{0,8},{8,0},{16,24},{24,16},{1,9},{9,1},{17,25},{25,17},{2,10},{10... | collective-permute-start | bytes 1032200 | tf_op jit(solution)/shard_map/ppermute | solution.py:601
  184.0 26.9 %collective-permute-start.6 = (f32[96,896]{1,0:T(8,128)}, f32[96,896]{1,0:T(8,128)}, u32[]{:S(2)}, u32[]{:S(2)}) collective-permute-start(f32[96,896]{1,0:T(8,128)} %get-tuple-element.35), channel_id=1, source_target_pairs={{0,16},{8,24},{16,0},{24,8},{1,17},{9,25},{17,1},{25,9},{2,18},{10... | collective-permute-start | bytes 1032200 | tf_op jit(solution)/shard_map/ppermute | solution.py:601
  186.3 24.6 %collective-permute-start.7 = (f32[96,896]{1,0:T(8,128)}, f32[96,896]{1,0:T(8,128)}, u32[]{:S(2)}, u32[]{:S(2)}) collective-permute-start(f32[96,896]{1,0:T(8,128)} %get-tuple-element.36), channel_id=1, source_target_pairs={{0,24},{8,16},{16,8},{24,0},{1,25},{9,17},{17,9},{25,1},{2,26},{10... | collective-permute-start | bytes 1032200 | tf_op jit(solution)/shard_map/ppermute | solution.py:601
  210.9 1.0 copy-start.2
  213.9 15.4 %collective-permute-start.8 = (f32[24,896]{1,0:T(8,128)}, f32[24,896]{1,0:T(8,128)S(1)}, u32[]{:S(2)}, u32[]{:S(2)}) collective-permute-start(f32[24,896]{1,0:T(8,128)} %get-tuple-element.38), channel_id=1, source_target_pairs={{0,2},{1,3},{2,0},{3,1},{4,6},{5,7},{6,4},{7,5},{8,10},{9,11},{10,... | collective-permute-start | bytes 258056 | tf_op jit(solution)/shard_map/ppermute | solution.py:608
  215.6 14.5 %collective-permute-start.9 = (f32[24,896]{1,0:T(8,128)}, f32[24,896]{1,0:T(8,128)S(1)}, u32[]{:S(2)}, u32[]{:S(2)}) collective-permute-start(f32[24,896]{1,0:T(8,128)} %get-tuple-element.39), channel_id=1, source_target_pairs={{0,4},{1,5},{2,6},{3,7},{4,0},{5,1},{6,2},{7,3},{8,12},{9,13},{10,... | collective-permute-start | bytes 258056 | tf_op jit(solution)/shard_map/ppermute | solution.py:608
  217.0 14.5 %copy-start.4 = (f32[24,896]{1,0:T(8,128)S(1)}, f32[24,896]{1,0:T(8,128)}, u32[]{:S(2)}) copy-start(f32[24,896]{1,0:T(8,128)} %get-tuple-element.37) | copy-start | bytes 258052
  217.0 14.5 %collective-permute-start.10 = (f32[24,896]{1,0:T(8,128)}, f32[24,896]{1,0:T(8,128)S(1)}, u32[]{:S(2)}, u32[]{:S(2)}) collective-permute-start(f32[24,896]{1,0:T(8,128)} %get-tuple-element.40), channel_id=1, source_target_pairs={{0,6},{1,7},{2,4},{3,5},{4,2},{5,3},{6,0},{7,1},{8,14},{9,15},{10,... | collective-permute-start | bytes 258056 | tf_op jit(solution)/shard_map/ppermute | solution.py:608
  231.6 41.5 %all-to-all-start.2 = ((bf16[8,1,6,64,512]{4,3,2,1,0:T(8,128)(2,1)}), bf16[8,1,6,64,512]{4,3,2,1,0:T(8,128)(2,1)S(1)}, u32[]{:S(2)}, u32[]{:S(2)}) async-start(bf16[8,1,6,64,512]{4,3,2,1,0:T(8,128)(2,1)} %rotate.2), calls=%async_computation.2 | async-start | bytes 6291456 | tf_op jit(solution)/shard_map/all_to_all | solution.py:699
